TPU v7x, 128 devices: a whole 4x4x4 slice. The times are simulated.
128 devices in a mesh: fsdp: 32 (over y, z, core), tensor: 4 (over x).
Axes of the slice: x: 4, y: 4, z: 4, core: 2. Of those that a mesh axis runs over, the one named last changes fastest.
Arguments:
- item_hidden: bfloat16 [65536, 4096], P('fsdp', 'tensor'), may hold values from -700 to 700
- item_gain: float32 [4096], P('tensor'), may hold values from 0.5 to 2
- occ_owner: int32 [8192, 1], P('fsdp'), may hold values from 0 to 31; in each aligned block of 256 rows (0 to 255, 256 to 511, ...) at most 16 rows name the same one
- occ_item: int32 [8192], P('fsdp'), may hold values from 0 to 255
- hist_len: int32 [32], P('fsdp'), may hold values from 128 to 256, as said below
- user_gain: float32 [4096], replicated, may hold values from 0.5 to 2
- wqkv: bfloat16 [3, 4096, 4096], P(None, 'fsdp', 'tensor'), may hold values from -2 to 2
- grad_out: bfloat16 [8192, 4096], P('fsdp', 'tensor'), may hold values from -6 to 6
Outputs:
- item_embed: bfloat16 [8192, 4096], P('fsdp', 'tensor')
- attn_out: bfloat16 [8192, 4096], P('fsdp', 'tensor')
- item_grads: float32 [8192, 4096], P('fsdp', 'tensor')
Inputs may be any that keep to these rules, and one draw needn't show every extreme that they name: `occ_owner`: among the 256 positions of one history, at most 16 name items of the same owner, a bound that some block reaches. `hist_len`: a multiple of 128; positions at or beyond it are padding; some history has the full 256.
All inputs are finite; a program needn't handle non-finite values.
Results may differ from a plain program's by a relative error of at most 0.022.
The roundings to bfloat16 on the way count: a program that leaves them out, or rounds other values in their place, can miss the bound.
Values may be sent and summed in bfloat16 or wider, within the bound.
A program may use at most 128 MiB of HBM per device.

v0:
```python
import math

import jax
import jax.numpy as jnp
from jax import lax
from jax.sharding import PartitionSpec as P

D = 4096
HEAD_DIM = 128
ITEM_LEN = 8


EPSILON = 1e-05


def attend(queries, key_rows, value_rows, upstream_in, length):
    extent = queries.shape[0]
    factor = 1.0 / math.sqrt(queries.shape[2])
    places = jnp.arange(extent, dtype=jnp.int32)
    allowed = (places[None, :] <= places[:, None]) & (places[None, :] < length)
    active = places < length
    scores = (
        jnp.einsum("qhe,khe->hqk", queries, key_rows, preferred_element_type=jnp.float32) * factor
    )
    scores = jnp.where(allowed[None], scores, jnp.float32(-1e30))
    row_max = jnp.max(scores, axis=2, keepdims=True)
    raised = jnp.where(allowed[None], jnp.exp(scores - row_max), jnp.float32(0.0))
    weights_f = raised / jnp.sum(raised, axis=2, keepdims=True)
    weights_b = weights_f.astype(jnp.bfloat16)
    attended = jnp.einsum("hqk,khe->qhe", weights_b, value_rows, preferred_element_type=jnp.float32)
    attended = jnp.where(active[:, None, None], attended, jnp.float32(0.0)).astype(jnp.bfloat16)
    upstream = jnp.where(active[:, None, None], upstream_in, jnp.zeros_like(upstream_in))
    grad_v = jnp.einsum(
        "hqk,qhe->khe", weights_b, upstream, preferred_element_type=jnp.float32
    ).astype(jnp.bfloat16)
    grad_p = jnp.einsum("qhe,khe->hqk", upstream, value_rows, preferred_element_type=jnp.float32)
    row_dot = jnp.sum(weights_f * grad_p, axis=2, keepdims=True)
    grad_s = (weights_f * (grad_p - row_dot) * factor).astype(jnp.bfloat16)
    grad_q = jnp.einsum(
        "hqk,khe->qhe", grad_s, key_rows, preferred_element_type=jnp.float32
    ).astype(jnp.bfloat16)
    grad_k = jnp.einsum("hqk,qhe->khe", grad_s, queries, preferred_element_type=jnp.float32).astype(
        jnp.bfloat16
    )
    return (attended, grad_q, grad_k, grad_v)


def on_device(item_hidden, item_gain, occ_owner, occ_item, hist_len, user_gain, wqkv, grad_out):
    values = item_hidden.astype(jnp.float32)
    partial_sq = jnp.sum(values * values, axis=1)
    total_sq = lax.psum(partial_sq, "tensor")
    inverse_item = lax.rsqrt(total_sq[:, None] / D + EPSILON)
    normed_items = values * inverse_item * item_gain
    local_items = normed_items.shape[0] // ITEM_LEN
    width = item_hidden.shape[1]
    item_embed = jnp.mean(normed_items.reshape(local_items, ITEM_LEN, width), axis=1).astype(
        jnp.bfloat16
    )
    owners = occ_owner[:, 0]
    extent = occ_item.shape[0]
    num_peers = lax.axis_size("fsdp")
    capacity = max(2, 2 * extent // num_peers)
    one_hot = (owners[:, None] == jnp.arange(num_peers, dtype=jnp.int32)[None, :]).astype(jnp.int32)
    ranking = jnp.cumsum(one_hot, axis=0) - 1
    within = jnp.sum(one_hot * ranking, axis=1)
    target = owners * capacity + within
    requests = (
        jnp.zeros((num_peers * capacity,), jnp.int32)
        .at[target]
        .set(occ_item)
        .reshape(num_peers, capacity)
    )
    asked = lax.all_to_all(requests, "fsdp", split_axis=0, concat_axis=0, tiled=True)
    found = item_embed[asked]
    fetched = lax.all_to_all(found, "fsdp", split_axis=0, concat_axis=0, tiled=True)
    gathered_share = fetched.reshape(num_peers * capacity, width)[target]
    gathered = lax.all_gather(gathered_share, "tensor", axis=1, tiled=True)
    inputs = gathered.astype(jnp.float32)
    inverse = lax.rsqrt(jnp.sum(inputs * inputs, axis=1, keepdims=True) / D + EPSILON)
    normed = (inputs * inverse * user_gain).astype(jnp.bfloat16)
    local_heads = width // HEAD_DIM
    w_full = lax.all_gather(wqkv, "fsdp", axis=1, tiled=True)
    projected = jnp.einsum("td,cde->cte", normed, w_full, preferred_element_type=jnp.float32)
    projected = projected.astype(jnp.bfloat16).reshape(3, extent, local_heads, HEAD_DIM)
    attended, grad_q, grad_k, grad_v = attend(
        projected[0],
        projected[1],
        projected[2],
        grad_out.reshape(extent, local_heads, HEAD_DIM),
        hist_len[0],
    )
    grads = jnp.stack([grad_q, grad_k, grad_v]).reshape(3, extent, width)
    head_terms = jnp.einsum("cte,cde->td", grads, w_full, preferred_element_type=jnp.float32)
    grad_normed = lax.psum(head_terms.astype(jnp.bfloat16), "tensor").astype(jnp.float32)
    scaled = grad_normed * user_gain
    row_stat = jnp.sum(inputs * scaled, axis=1, keepdims=True) / D
    grad_full = inverse * scaled - inputs * inverse**3 * row_stat
    grad_in = lax.dynamic_slice_in_dim(grad_full, lax.axis_index("tensor") * width, width, 1)
    grad_in = grad_in.astype(jnp.bfloat16)
    outgoing = (
        jnp.zeros((num_peers * capacity, width), jnp.bfloat16)
        .at[target]
        .set(grad_in)
        .reshape(num_peers, capacity, width)
    )
    incoming = lax.all_to_all(outgoing, "fsdp", split_axis=0, concat_axis=0, tiled=True)
    matches = (
        asked.reshape(-1)[:, None] == jnp.arange(local_items, dtype=jnp.int32)[None, :]
    ).astype(jnp.bfloat16)
    item_grads = jnp.einsum(
        "si,sd->id", matches, incoming.reshape(-1, width), preferred_element_type=jnp.float32
    )
    return (item_embed, attended.reshape(extent, width), item_grads)


def solution(mesh):
    in_specs = (
        P("fsdp", "tensor"),
        P("tensor"),
        P("fsdp", None),
        P("fsdp"),
        P("fsdp"),
        P(),
        P(None, "fsdp", "tensor"),
        P("fsdp", "tensor"),
    )
    out_specs = (P("fsdp", "tensor"), P("fsdp", "tensor"), P("fsdp", "tensor"))
    return jax.shard_map(
        on_device, mesh=mesh, in_specs=in_specs, out_specs=out_specs, check_vma=False
    )
```

profile of v0, /device:TPU:1, one launch (start us, length us, event | category | flops | bytes accessed | tf_op | source)
XLA Modules:
  0.0 343.9 jit_solution(17610707857865834671)
XLA Ops:
  7.2 0.7 fusion.68
  7.9 0.6 reduce-window.6
  8.4 0.2 slice_reduce_fusion
  8.7 0.8 fusion.67
  9.4 0.7 compare_select_fusion.1
  10.1 1.6 scatter_custom_fusion
  11.7 0.7 all_to_all.14
  12.4 9.6 %all-to-all-start = ((s32[32,1,16]{2,1,0:T(1,128)}), s32[32,1,16]{2,1,0:T(1,128)S(1)}, u32[]{:S(2)}, u32[]{:S(2)}) async-start(s32[32,1,16]{2,1,0:T(1,128)} %bitcast.7), calls=%async_computation | async-start | bytes 32768 | tf_op jit(solution)/shard_map/all_to_all | solution.py:73
  22.0 3.1 fusion.2
  25.1 8.6 %psum.14 = f32[2048]{0:T(1024)S(1)} all-reduce(f32[2048]{0:T(1024)S(1)} %fusion.2), channel_id=1, replica_groups=mesh['fsdp'=32,'tensor'=4] {'tensor'}, use_global_device_ids=true, to_apply=%region_1.0 | all-reduce | flops 2048 | bytes 16384 | tf_op jit(solution)/shard_map/psum | solution.py:51
  33.7 4.6 %fusion.5 = f32[256,1024]{1,0:T(8,128)S(1)} fusion(bf16[2048,1024]{1,0:T(8,128)(2,1)} %param.8, f32[1024]{0:T(1024)S(1)} %copy-done.4, f32[2048]{0:T(1024)S(1)} %add_rsqrt_fusion), kind=kLoop, calls=%fused_computation.11 | loop fusion | flops 8126464 | bytes 5255168 | tf_op jit(solution)/shard_map/reduce_sum | solution.py:56
  38.2 0.1 multiply_convert_fusion.2
  38.4 0.1 reshape.163
  38.5 2.8 gather_fusion
  41.2 9.4 %all-to-all-start.1 = ((bf16[32,16,1024]{2,1,0:T(8,128)(2,1)}), bf16[32,16,1024]{2,1,0:T(8,128)(2,1)S(1)}, u32[]{:S(2)}, u32[]{:S(2)}) async-start(bf16[32,16,1024]{2,1,0:T(8,128)(2,1)} %bitcast.9), calls=%async_computation.1 | async-start | bytes 2097152 | tf_op jit(solution)/shard_map/all_to_all | solution.py:75
  50.7 16.9 %all-to-all-done.1 = bf16[32,16,1024]{2,1,0:T(8,128)(2,1)S(1)} async-done(((bf16[32,16,1024]{2,1,0:T(8,128)(2,1)}), bf16[32,16,1024]{2,1,0:T(8,128)(2,1)S(1)}, u32[]{:S(2)}, u32[]{:S(2)}) %all-to-all-start.1) | async-done | bytes 1048608 | tf_op jit(solution)/shard_map/all_to_all | solution.py:75
  67.6 2.0 gather_fusion.1
  69.6 0.7 all-gather.4.cloned.1.call-update
  71.0 0.2 copy.67
  71.2 0.1 fusion.63
  71.3 24.6 %all-gather.6.cloned.1.call-done = bf16[256,4096]{1,0:T(8,128)(2,1)} async-done(((bf16[256,1024]{1,0:T(8,128)(2,1)}), bf16[256,4096]{1,0:T(8,128)(2,1)}) %all-gather.6.cloned.1.call-update) | async-done | bytes 2097168 | tf_op jit(solution)/shard_map/all_gather | solution.py:77
  95.9 2.2 multiply_reduce_fusion.1
  98.1 92.9 %all-gather.4.cloned.1.call-done = bf16[3,4096,1024]{2,1,0:T(8,128)(2,1)} async-done(((bf16[3,128,1024]{2,1,0:T(8,128)(2,1)}), bf16[3,4096,1024]{2,1,0:T(8,128)(2,1)}) %all-gather.4.cloned.1.call-update) | async-done | bytes 25165840 | tf_op jit(solution)/shard_map/all_gather | solution.py:82
  191.0 11.9 %fusion.30 = bf16[3,256,1024]{2,1,0:T(8,128)(2,1)S(1)} fusion(bf16[3,4096,1024]{2,1,0:T(8,128)(2,1)} %all-gather.4.cloned.1.call-done, bf16[256,4096]{1,0:T(8,128)(2,1)S(1)} %copy-done.1, f32[4096]{0:T(1024)S(1)} %copy-done.3, f32[256]{0:T(256)S(1)} %get-tuple-element.18), kind=kOutput, calls=%fused_computation.36 | convolution fusion | flops 6447431680 | bytes 28853248 | tf_op jit(solution)/shard_map/td,cde->cte/dot_general | solution.py:83
  203.0 1.1 fusion.80
  204.0 2.1 copy.68
  206.1 1.0 copy.69
  207.1 1.1 copy.71
  208.2 1.7 fusion.58
  210.0 3.6 %fusion.81 = (f32[8,256]{1,0:T(8,128)S(1)}, f32[8,256,256]{1,2,0:T(8,128)}) fusion(pred[256,256]{0,1:T(8,128)(4,1)S(1)} %fusion.63, bf16[256,8,128]{0,2,1:T(8,128)(2,1)} %bitcast.78, bf16[256,8,128]{0,2,1:T(8,128)(2,1)} %bitcast.80), kind=kOutput, calls=%fused_computation.103 | convolution fusion | flops 136839424 | bytes 3219456 | tf_op jit(solution)/shard_map/sub | solution.py:27
  213.6 5.3 %fusion.34 = bf16[8,128,256]{2,1,0:T(8,128)(2,1)} fusion(bf16[256,8,128]{0,2,1:T(8,128)(2,1)} %bitcast.81, f32[8,256,256]{1,2,0:T(8,128)} %fusion.58, f32[8,256,256]{1,2,0:T(8,128)} %get-tuple-element.20, f32[8,256]{1,0:T(8,128)S(1)} %get-tuple-element.19), kind=kOutput, calls=%fused_computation.39 | convolution fusion | flops 138152192 | bytes 5251072 | tf_op jit(solution)/shard_map/hqk,khe->qhe/dot_general | solution.py:39
  218.9 5.2 %fusion.37 = bf16[8,128,256]{2,1,0:T(8,128)(2,1)} fusion(bf16[256,8,128]{0,2,1:T(8,128)(2,1)} %bitcast.79, f32[8,256,256]{1,2,0:T(8,128)} %fusion.58, f32[8,256,256]{1,2,0:T(8,128)} %get-tuple-element.20, f32[8,256]{1,0:T(8,128)S(1)} %get-tuple-element.19), kind=kOutput, calls=%fused_computation.40 | convolution fusion | flops 138152192 | bytes 5251072 | tf_op jit(solution)/shard_map/hqk,qhe->khe/dot_general | solution.py:42
  224.1 2.9 convolution_convert_fusion
  227.0 1.2 copy.58
  228.2 2.1 copy.59
  230.3 2.0 copy.60
  232.4 12.9 %fusion.6 = bf16[256,4096]{1,0:T(8,128)(2,1)} fusion(bf16[3,4096,1024]{2,1,0:T(8,128)(2,1)} %all-gather.4.cloned.1.call-done, bf16[1,256,1024]{2,1,0:T(8,128)(2,1)} %copy.60, bf16[1,256,1024]{2,1,0:T(8,128)(2,1)} %copy.59, bf16[1,256,1024]{2,1,0:T(8,128)(2,1)S(1)} %copy.58), kind=kOutput, calls=%fused_computation.13 | convolution fusion | flops 6445072384 | bytes 28835840 | tf_op jit(solution)/shard_map/cte,cde->td/dot_general | solution.py:93
  245.3 2.4 convert_element_type.66
  247.7 55.3 %all-reduce.2.cloned.1.call-done = bf16[256,4096]{1,0:T(8,128)(2,1)} async-done(((bf16[256,4096]{1,0:T(8,128)(2,1)}), bf16[256,4096]{1,0:T(8,128)(2,1)}) %all-reduce.2.cloned.1.call-update) | async-done | bytes 2097168 | tf_op jit(solution)/shard_map/psum | solution.py:94
  302.9 4.2 %multiply_reduce_fusion = (f32[256]{0:T(256)S(1)}, f32[256,4096]{1,0:T(8,128)}) fusion(bf16[256,4096]{1,0:T(8,128)(2,1)S(1)} %copy-done.1, f32[4096]{0:T(1024)S(1)} %copy-done.3, bf16[256,4096]{1,0:T(8,128)(2,1)} %all-reduce.2.cloned.1.call-done), kind=kLoop, calls=%fused_computation.14 | loop fusion | flops 5242624 | bytes 8406016 | tf_op jit(solution)/shard_map/reduce_sum | solution.py:96
  307.2 4.0 %scatter_custom_fusion.1 = bf16[512,1024]{1,0:T(8,128)(2,1)} fusion(s32[256]{0:T(256)S(1)} %bitcast.91, f32[256,4096]{1,0:T(8,128)} %get-tuple-element.13, s32[]{:T(128)} %constant.20.clone.1, s32[]{:T(128)S(6)} %select_n.41, f32[256,4096]{1,0:T(8,128)} %convert_element_type.66, f32[256]{0:T(256)S(1)} %broadcast_multiply_fusion, ...), kind=kCustom, calls=%fused_computation.54 | custom fusion | flops 1310720 | bytes 3149828 | tf_op jit(solution)/shard_map/scatter | solution.py:103
  311.2 7.7 %all-to-all-start.2 = ((bf16[32,16,1024]{2,1,0:T(8,128)(2,1)}), bf16[32,16,1024]{2,1,0:T(8,128)(2,1)S(1)}, u32[]{:S(2)}, u32[]{:S(2)}) async-start(bf16[32,16,1024]{2,1,0:T(8,128)(2,1)} %bitcast.23), calls=%async_computation.2 | async-start | bytes 2097152 | tf_op jit(solution)/shard_map/all_to_all | solution.py:106
  318.9 0.5 broadcast.152
  319.4 0.7 reduce.5
  320.2 2.0 fusion.33
  322.2 1.0 copy.61
  323.2 12.7 %all-to-all-done.2 = bf16[32,16,1024]{2,1,0:T(8,128)(2,1)S(1)} async-done(((bf16[32,16,1024]{2,1,0:T(8,128)(2,1)}), bf16[32,16,1024]{2,1,0:T(8,128)(2,1)S(1)}, u32[]{:S(2)}, u32[]{:S(2)}) %all-to-all-start.2) | async-done | bytes 1048608 | tf_op jit(solution)/shard_map/all_to_all | solution.py:106
  335.8 1.6 fusion.56
  (26 shorter events, 0.4 us)
Async XLA Ops:
  12.4 26.0 %all-to-all-start = ((s32[32,1,16]{2,1,0:T(1,128)}), s32[32,1,16]{2,1,0:T(1,128)S(1)}, u32[]{:S(2)}, u32[]{:S(2)}) async-start(s32[32,1,16]{2,1,0:T(1,128)} %bitcast.7), calls=%async_computation | async-start | bytes 32768 | tf_op jit(solution)/shard_map/all_to_all | solution.py:73
  22.0 11.7 %copy-start.4 = (f32[1024]{0:T(1024)S(1)}, f32[1024]{0:T(1024)}, u32[]{:S(2)}) copy-start(f32[1024]{0:T(1024)} %param.9) | copy-start | bytes 12292
  38.3 2.9 copy-start
  41.2 26.3 %all-to-all-start.1 = ((bf16[32,16,1024]{2,1,0:T(8,128)(2,1)}), bf16[32,16,1024]{2,1,0:T(8,128)(2,1)S(1)}, u32[]{:S(2)}, u32[]{:S(2)}) async-start(bf16[32,16,1024]{2,1,0:T(8,128)(2,1)} %bitcast.9), calls=%async_computation.1 | async-start | bytes 2097152 | tf_op jit(solution)/shard_map/all_to_all | solution.py:75
  50.6 45.2 %all-gather.6.cloned.1.call-start = ((), (), s32[]{:S(2)}) async-start(), calls=%async_computation.5 | async-start | bytes 2621440 | tf_op jit(solution)/shard_map/all_gather | solution.py:77
  67.6 3.4 %copy-start.2 = (bf16[256,1024]{1,0:T(8,128)(2,1)S(1)}, bf16[256,1024]{1,0:T(8,128)(2,1)}, u32[]{:S(2)}) copy-start(bf16[256,1024]{1,0:T(8,128)(2,1)} %param.15) | copy-start | bytes 1572868
  69.5 121.5 %copy-start.3 = (f32[4096]{0:T(1024)S(1)}, f32[4096]{0:T(1024)}, u32[]{:S(2)}) copy-start(f32[4096]{0:T(1024)} %param.13) | copy-start | bytes 49156
  69.5 121.5 %all-gather.4.cloned.1.call-start = ((), (), s32[]{:S(2)}) async-start(), calls=%async_computation.3 | async-start | bytes 25952256 | tf_op jit(solution)/shard_map/all_gather | solution.py:82
  70.3 232.6 %all-reduce.2.cloned.1.call-start = ((), (), s32[]{:S(2)}) async-start(), calls=%async_computation.4 | async-start | bytes 4194304 | tf_op jit(solution)/shard_map/psum | solution.py:94
  95.9 95.1 %copy-start.1 = (bf16[256,4096]{1,0:T(8,128)(2,1)S(1)}, bf16[256,4096]{1,0:T(8,128)(2,1)}, u32[]{:S(2)}) copy-start(bf16[256,4096]{1,0:T(8,128)(2,1)} %all-gather.6.cloned.1.call-done) | copy-start | bytes 6291460
  311.2 24.6 %all-to-all-start.2 = ((bf16[32,16,1024]{2,1,0:T(8,128)(2,1)}), bf16[32,16,1024]{2,1,0:T(8,128)(2,1)S(1)}, u32[]{:S(2)}, u32[]{:S(2)}) async-start(bf16[32,16,1024]{2,1,0:T(8,128)(2,1)} %bitcast.23), calls=%async_computation.2 | async-start | bytes 2097152 | tf_op jit(solution)/shard_map/all_to_all | solution.py:106
Sparse Core Ops, SparseCore 0:
  69.7 26.1 all-gather.5
  98.3 92.7 all-gather.3
  245.4 57.5 all-reduce.1
where the time goes:
time: 345 us; the launch traced here: 344 us
  waiting for transfers between devices  203 us (59%)
  matrix products  47.1 us (14%)
  starting transfers between devices  26.8 us (8%)
  other arithmetic  24.2 us (7%)
  local copies, waits for them, and re-layouts  19.7 us (6%)
  between operations  14.6 us (4%)
  blocking collectives  8.58 us (2%)
    all_gather x1, waiting for transfers between devices, on_device(): w_full = lax.all_gather(wqkv, 'fsdp', axis=1, tiled=True)  92.9 us
    psum x1, waiting for transfers between devices, on_device(): lax.psum(head_terms.astype(jnp.bfloat16), 'tensor').astype(jnp.float32)  55.3 us
    all_gather x1, waiting for transfers between devices, on_device(): gathered = lax.all_gather(gathered_share, 'tensor', axis=1, tiled=True)  24.6 us
    all_to_all x1, waiting for transfers between devices, on_device(): lax.all_to_all(found, 'fsdp', split_axis=0, concat_axis=0, tiled=True)  16.9 us
    dot_general x1, matrix products, on_device(): jnp.einsum('cte,cde->td', grads, w_full, preferred_element_type=jnp.float32)  12.9 us
    all_to_all x1, waiting for transfers between devices, on_device(): lax.all_to_all(outgoing, 'fsdp', split_axis=0, concat_axis=0, tiled=True)  12.7 us
    dot_general x1, matrix products, on_device(): jnp.einsum('td,cde->cte', normed, w_full, preferred_element_type=jnp.floa...  11.9 us
    all_to_all x1, starting transfers between devices, on_device(): lax.all_to_all(requests, 'fsdp', split_axis=0, concat_axis=0, tiled=True)  9.6 us
  transfers between devices with their start and end apart: 6, of which 5 were waited for; matrix products, arithmetic and copies ran while one was open for 5% of the time, Pallas kernels for 0%

commit v1 on v0

v1 whole, which is shorter than its diff:
```python
import functools
import math

import jax
import jax.numpy as jnp
from jax import lax
from jax.experimental import pallas as pl
from jax.experimental.pallas import tpu as pltpu
from jax.sharding import PartitionSpec as P

D = 4096
HEAD_DIM = 128
ITEM_LEN = 8
EPSILON = 1e-05
NF = 32
NX = 4
ROWS = 256
CAP = 16
SLOTS = NF * CAP
WIDTH = D // NX
HALF = WIDTH // 2
SHARD = D // NF
F32 = jnp.float32
BF16 = jnp.bfloat16
MIB = 1 << 20


def rcopy(src, dst, send, recv, **where):
    copy = pltpu.make_async_remote_copy(
        src_ref=src,
        dst_ref=dst,
        send_sem=send,
        recv_sem=recv,
        device_id=where,
        device_id_type=pl.DeviceIdType.MESH,
    )
    copy.start()
    return copy


def arrived(ref, sem):
    pltpu.make_async_copy(ref, ref, sem).wait()


def greet():
    f, x = lax.axis_index("fsdp"), lax.axis_index("tensor")
    barrier = pltpu.get_barrier_semaphore()

    def signal(d, carry):
        pl.semaphore_signal(
            barrier,
            inc=1,
            device_id={"fsdp": lax.rem(f + d, NF)},
            device_id_type=pl.DeviceIdType.MESH,
        )
        return carry

    lax.fori_loop(1, NF, signal, 0)
    for d in range(1, NX):
        pl.semaphore_signal(
            barrier,
            inc=1,
            device_id={"tensor": lax.rem(x + d, NX)},
            device_id_type=pl.DeviceIdType.MESH,
        )
    pl.semaphore_wait(barrier, NF - 1 + NX - 1)


def front_kernel(
    hid, gain, w, ids, g,
    xh, wo, emb_o, oh_o, tt_o, pair_o, g_o,
    hid_v, idb, sqb, inv_v, fnd, fet, share,
    loc, id_s, id_r, sq_s, sq_r, a_s, a_r, w_s, w_r, w_r2, x_s, x_r, x_r2, p_s, p_r, m_s, m_r,
):
    f, x = lax.axis_index("fsdp"), lax.axis_index("tensor")
    c = lax.rem(f, 2)
    chip = f // 2
    z, y = lax.rem(chip, 4), chip // 4
    mate = f + 1 - 2 * c
    idx = lambda yy, zz, cc: (yy * 4 + zz) * 2 + cc
    y1, y2, y3 = (lax.rem(y + d, 4) for d in (1, 2, 3))
    z1, z2, z3 = (lax.rem(z + d, 4) for d in (1, 2, 3))
    x1, x2, x3 = (lax.rem(x + d, 4) for d in (1, 2, 3))
    yp, ym, zp, zm = idx(y1, z, c), idx(y3, z, c), idx(y, z1, c), idx(y, z3, c)

    load_hid = pltpu.make_async_copy(hid, hid_v, loc.at[0])
    load_hid.start()
    own_cols = pl.ds(pl.multiple_of(c * HALF, HALF), HALF)
    mate_cols = pl.ds(pl.multiple_of((1 - c) * HALF, HALF), HALF)

    def block(b):
        return wo.at[:, pl.ds(pl.multiple_of(b * SHARD, SHARD), SHARD), :]

    def part(b, h):
        at = pl.multiple_of(b * SHARD + h * (SHARD // 2), SHARD // 2)
        return wo.at[:, pl.ds(at, SHARD // 2), :]

    keep_w = pltpu.make_async_copy(w.at[:, :, own_cols], block(f), loc.at[1])
    keep_w.start()
    keep_id = pltpu.make_async_copy(ids, idb.at[f], loc.at[2])
    keep_id.start()
    keep_g = pltpu.make_async_copy(g.at[:, own_cols], g_o.at[c], loc.at[3])
    keep_g.start()

    greet()

    sends = []
    wcount = [0]

    def wsend(src, dst, recv, dev):
        sends.append(rcopy(src, dst, w_s.at[wcount[0]], recv, fsdp=dev))
        wcount[0] += 1

    def full(b, dev):
        wsend(block(b), block(b), w_r.at[b], dev)

    def half(b, h, dev):
        wsend(part(b, h), part(b, h), (w_r if h == 0 else w_r2).at[b], dev)

    def got(b):
        arrived(block(b), w_r.at[b])

    def got_halves(b):
        arrived(part(b, 0), w_r.at[b])
        arrived(part(b, 1), w_r2.at[b])

    wsend(w.at[:, :, mate_cols], block(f), w_r.at[f], mate)
    for dev in (yp, ym, zp, zm):
        wsend(w.at[:, :, own_cols], block(f), w_r.at[f], dev)

    def id_send(d, carry):
        to = lax.rem(f + d, NF)
        rcopy(ids, idb.at[f], id_s.at[to], id_r.at[f], fsdp=to)
        return carry

    lax.fori_loop(1, NF, id_send, 0)
    sends.append(rcopy(g.at[:, mate_cols], g_o.at[c], m_s, m_r, fsdp=mate))

    load_hid.wait()
    lane = lax.broadcasted_iota(jnp.int32, (128, 128), 1)

    def squares(k, acc):
        v = hid_v[pl.ds(pl.multiple_of(k * 128, 128), 128), :].astype(F32)
        return jnp.where(lane == k, jnp.sum(v * v, axis=1, keepdims=True), acc)

    sqb[x] = lax.fori_loop(0, 16, squares, jnp.zeros((128, 128), F32))
    for n, to in enumerate((x1, x3, x2)):
        sends.append(rcopy(sqb.at[x], sqb.at[x], sq_s.at[n], sq_r.at[x], tensor=to))

    got(mate)
    for dev in (yp, ym, zp, zm):
        full(mate, dev)

    def id_wait(d, carry):
        frm = lax.rem(f + d, NF)
        arrived(idb.at[frm], id_r.at[frm])
        return carry

    lax.fori_loop(1, NF, id_wait, 0)
    keep_id.wait()
    pair_o[c] = idb[f]
    pair_o[1 - c] = idb[mate]
    row = lax.broadcasted_iota(jnp.int32, (SLOTS, ROWS), 0)
    col = lax.broadcasted_iota(jnp.int32, (SLOTS, ROWS), 1)
    slot = lax.rem(row, CAP).astype(F32)
    group = row // CAP
    before = (
        lax.broadcasted_iota(jnp.int32, (ROWS, ROWS), 0) < lax.broadcasted_iota(jnp.int32, (ROWS, ROWS), 1)
    ).astype(F32).astype(BF16)

    def slots_of(named):
        rank = jnp.dot(named.astype(F32).astype(BF16), before, preferred_element_type=F32)
        return named & (rank == slot)

    mine_owner = jnp.broadcast_to(idb[f, 0:1, :], (SLOTS, ROWS))
    tt_o[...] = slots_of(mine_owner == group).astype(F32).astype(BF16)
    table = idb[...].reshape(NF * 8, ROWS).astype(F32).astype(BF16)
    pick_owner = (col == group * 8).astype(F32).astype(BF16)
    pick_item = (col == group * 8 + 1).astype(F32).astype(BF16)
    owner_all = jnp.dot(pick_owner, table, preferred_element_type=F32)
    item_all = jnp.dot(pick_item, table, preferred_element_type=F32)
    taken = slots_of(owner_all == f.astype(F32))
    wanted = jnp.sum(jnp.where(taken, item_all + 1.0, 0.0), axis=1, keepdims=True) - 1.0
    oh_o[...] = (wanted == col.astype(F32)).astype(F32).astype(BF16)

    for frm in (x1, x3, x2):
        arrived(sqb.at[frm], sq_r.at[frm])
    inv_v[...] = lax.rsqrt((sqb[0] + sqb[1] + sqb[2] + sqb[3]) / D + EPSILON)

    def pool(k, carry):
        v = hid_v[pl.ds(pl.multiple_of(k * 128, 128), 128), :].astype(F32)
        inv = jnp.sum(jnp.where(lane == k, inv_v[...], 0.0), axis=1, keepdims=True)
        total = jnp.sum((v * inv).reshape(16, ITEM_LEN, WIDTH), axis=1)
        emb_o[pl.ds(pl.multiple_of(k * 16, 16), 16), :] = (
            total * (1.0 / ITEM_LEN) * gain[...]
        ).astype(BF16)
        return carry

    lax.fori_loop(0, 16, pool, 0)
    fnd[...] = jnp.dot(oh_o[...], emb_o[...], preferred_element_type=F32).astype(BF16)

    def slot_rows(b):
        return pl.ds(pl.multiple_of(b * CAP, CAP), CAP)

    def a_send(d, carry):
        to = lax.rem(f + d, NF)
        rcopy(fnd.at[slot_rows(to)], fet.at[slot_rows(f)], a_s.at[to], a_r.at[f], fsdp=to)
        return carry

    lax.fori_loop(1, NF, a_send, 0)
    fet[slot_rows(f), :] = fnd[slot_rows(f), :]

    for r, prev, nxt, dn, up in ((0, idx(y3, z, 0), idx(y1, z, 0), ym, yp), (1, idx(y, z3, 1), idx(y, z1, 1), zm, zp)):
        got(prev)
        half(prev, 0, up)
        got(nxt)
        half(nxt, 1, dn)
    for dev in (zp, zm):
        full(idx(y3, z, 0), dev)
        full(idx(y1, z, 0), dev)
    for dev in (yp, ym):
        full(idx(y, z3, 1), dev)
        full(idx(y, z1, 1), dev)
    got_halves(idx(y2, z, 0))
    for dev in (zp, zm):
        full(idx(y2, z, 0), dev)
    got_halves(idx(y, z2, 1))
    for dev in (yp, ym):
        full(idx(y, z2, 1), dev)

    def a_wait(d, carry):
        frm = lax.rem(f + d, NF)
        arrived(fet.at[slot_rows(frm)], a_r.at[frm])
        return carry

    lax.fori_loop(1, NF, a_wait, 0)
    share[...] = lax.dot_general(
        tt_o[...], fet[...], (((0,), (0,)), ((), ())), preferred_element_type=F32
    ).astype(BF16)

    def cols(j):
        return pl.ds(pl.multiple_of(j * WIDTH, WIDTH), WIDTH)

    def piece(j, h):
        return xh.at[c, pl.ds(h * (ROWS // 2), ROWS // 2), cols(j)]

    keep_x = pltpu.make_async_copy(share, xh.at[c, :, cols(x)], loc.at[4])
    keep_x.start()
    sends.append(rcopy(share, xh.at[c, :, cols(x)], x_s.at[0], x_r.at[x], tensor=x1))
    sends.append(rcopy(share, xh.at[c, :, cols(x)], x_s.at[1], x_r.at[x], tensor=x3))
    sends.append(rcopy(share, xh.at[c, :, cols(x)], p_s.at[0], p_r.at[x], fsdp=mate))

    for n, (yy, zz) in enumerate(zip((y, y3, y1, y2), (z, z3, z1, z2))):
        got(idx(yy, z3, 0))
        half(idx(yy, z3, 0), 0, zp)
        got(idx(yy, z1, 0))
        half(idx(yy, z1, 0), 1, zm)
        got(idx(y3, zz, 1))
        half(idx(y3, zz, 1), 0, yp)
        got(idx(y1, zz, 1))
        half(idx(y1, zz, 1), 1, ym)
        if n == 0:
            for h, (frm, to) in enumerate(((x3, x1), (x1, x3))):
                arrived(xh.at[c, :, cols(frm)], x_r.at[frm])
                recv = (x_r if h == 0 else x_r2).at[frm]
                sends.append(rcopy(piece(frm, h), piece(frm, h), x_s.at[2 + h], recv, tensor=to))
                whole = xh.at[c, :, cols(frm)]
                sends.append(rcopy(whole, whole, p_s.at[1 + h], p_r.at[frm], fsdp=mate))

    arrived(piece(x2, 0), x_r.at[x2])
    arrived(piece(x2, 1), x_r2.at[x2])
    whole = xh.at[c, :, cols(x2)]
    sends.append(rcopy(whole, whole, p_s.at[3], p_r.at[x2], fsdp=mate))
    for j in (x, x3, x1, x2):
        arrived(xh.at[1 - c, :, cols(j)], p_r.at[j])
    keep_x.wait()

    for yy in (y, y1, y2, y3):
        got_halves(idx(yy, z2, 0))
    for zz in (z, z1, z2, z3):
        got_halves(idx(y2, zz, 1))
    arrived(g_o.at[1 - c], m_r)
    keep_w.wait()
    keep_g.wait()
    for copy in sends:
        copy.wait_send()

    def settle(d, carry):
        to = lax.rem(f + d, NF)
        pltpu.make_async_copy(ids, ids, id_s.at[to]).wait()
        pltpu.make_async_copy(fnd.at[slot_rows(to)], fnd.at[slot_rows(to)], a_s.at[to]).wait()
        return carry

    lax.fori_loop(1, NF, settle, 0)


ANY = pl.BlockSpec(memory_space=pl.ANY)
VMEM = pl.BlockSpec(memory_space=pltpu.VMEM)
DMA = pltpu.SemaphoreType.DMA


def front(item_hidden, item_gain, wqkv, ids, grad_out):
    return pl.pallas_call(
        front_kernel,
        out_shape=(
            jax.ShapeDtypeStruct((2, ROWS, D), BF16),
            jax.ShapeDtypeStruct((3, D, HALF), BF16),
            jax.ShapeDtypeStruct((ROWS, WIDTH), BF16),
            jax.ShapeDtypeStruct((SLOTS, ROWS), BF16),
            jax.ShapeDtypeStruct((SLOTS, ROWS), BF16),
            jax.ShapeDtypeStruct((2, 8, ROWS), jnp.int32),
            jax.ShapeDtypeStruct((2, ROWS, HALF), BF16),
        ),
        in_specs=[ANY, VMEM, ANY, ANY, ANY],
        out_specs=(ANY, ANY, VMEM, VMEM, VMEM, VMEM, ANY),
        scratch_shapes=[
            pltpu.VMEM((ROWS * ITEM_LEN, WIDTH), BF16),
            pltpu.VMEM((NF, 8, ROWS), jnp.int32),
            pltpu.VMEM((NX, 128, 128), F32),
            pltpu.VMEM((128, 128), F32),
            pltpu.VMEM((SLOTS, WIDTH), BF16),
            pltpu.VMEM((SLOTS, WIDTH), BF16),
            pltpu.VMEM((ROWS, WIDTH), BF16),
            DMA((5,)),
            DMA((NF,)), DMA((NF,)),
            DMA((3,)), DMA((NX,)),
            DMA((NF,)), DMA((NF,)),
            DMA((41,)), DMA((NF,)), DMA((NF,)),
            DMA((4,)), DMA((NX,)), DMA((NX,)),
            DMA((4,)), DMA((NX,)),
            DMA, DMA,
        ],
        compiler_params=pltpu.CompilerParams(
            collective_id=0, has_side_effects=True, vmem_limit_bytes=48 * MIB
        ),
        cost_estimate=pl.CostEstimate(flops=10**9, bytes_accessed=64 * MIB, transcendentals=0),
        name="front",
    )(item_hidden, item_gain, wqkv, ids, grad_out)


def core_kernel(
    xh, gain, pair, g, w,
    attn, dx, inv_o, stat,
    wv, nrm, acc, qkv, grads, sem,
):
    loads = [pltpu.make_async_copy(w.at[n], wv.at[n], sem.at[n]) for n in range(3)]
    for load in loads:
        load.start()

    def norm(k, carry):
        rows = pl.ds(pl.multiple_of(k * 32, 32), 32)
        v = xh[rows, :].astype(F32)
        inv = lax.rsqrt(jnp.sum(v * v, axis=1, keepdims=True) / D + EPSILON)
        nrm[rows, :] = (v * inv * gain[...]).astype(BF16)
        inv_o[rows, :] = jnp.broadcast_to(inv, (32, 128))
        return carry

    lax.fori_loop(0, 16, norm, 0)

    steps = 4
    depth = D // steps
    for n in range(3):
        loads[n].wait()

        def project(k, carry):
            at = pl.ds(pl.multiple_of(k * depth, depth), depth)
            acc[...] += jnp.dot(nrm[:, at], wv[n, at, :], preferred_element_type=F32)
            return carry

        acc[...] = jnp.zeros_like(acc)
        lax.fori_loop(0, steps, project, 0)
        qkv[n] = acc[...].astype(BF16)

    factor = 1.0 / math.sqrt(HEAD_DIM)
    heads = HALF // HEAD_DIM
    t_at = lax.broadcasted_iota(jnp.int32, (ROWS, ROWS), 0)
    s_at = lax.broadcasted_iota(jnp.int32, (ROWS, ROWS), 1)
    t_row = lax.broadcasted_iota(jnp.int32, (ROWS, HEAD_DIM), 0)
    nt = (((1,), (1,)), ((), ()))
    tn = (((0,), (0,)), ((), ()))

    def attend(k, carry):
        h, n = k // heads, lax.rem(k, heads)
        rows = pl.ds(pl.multiple_of(h * ROWS, ROWS), ROWS)
        cols = pl.ds(pl.multiple_of(n * HEAD_DIM, HEAD_DIM), HEAD_DIM)
        length = pair[h, 2:3, :]
        allowed = (s_at <= t_at) & (s_at < length)
        live = t_row < length[:, :HEAD_DIM]
        qq, kk, vv = qkv[0, rows, cols], qkv[1, rows, cols], qkv[2, rows, cols]
        gg = jnp.where(live, g[h, :, cols].astype(F32), 0.0).astype(BF16)
        scores = lax.dot_general(qq, kk, nt, preferred_element_type=F32) * factor
        scores = jnp.where(allowed, scores, -1e30)
        top = jnp.max(scores, axis=1, keepdims=True)
        raised = jnp.where(allowed, jnp.exp(scores - top), 0.0)
        probs = raised * (1.0 / jnp.sum(raised, axis=1, keepdims=True))
        pb = probs.astype(BF16)
        out = jnp.dot(pb, vv, preferred_element_type=F32)
        attn[rows, cols] = jnp.where(live, out, 0.0).astype(BF16)
        dv = lax.dot_general(pb, gg, tn, preferred_element_type=F32).astype(BF16)
        dp = lax.dot_general(gg, vv, nt, preferred_element_type=F32)
        mid = jnp.sum(probs * dp, axis=1, keepdims=True)
        ds = (probs * (dp - mid) * factor).astype(BF16)
        dq = jnp.dot(ds, kk, preferred_element_type=F32).astype(BF16)
        dk = lax.dot_general(ds, qq, tn, preferred_element_type=F32).astype(BF16)
        grads[0, rows, cols] = dq
        grads[1, rows, cols] = dk
        grads[2, rows, cols] = dv
        terms = (
            dq.astype(F32) * qq.astype(F32)
            + dk.astype(F32) * kk.astype(F32)
            + dv.astype(F32) * vv.astype(F32)
        )
        stat[rows, :] += jnp.broadcast_to(jnp.sum(terms, axis=1, keepdims=True), (ROWS, 128))
        return carry

    stat[...] = jnp.zeros_like(stat)
    lax.fori_loop(0, 2 * heads, attend, 0)

    def back(k, carry):
        at = pl.ds(pl.multiple_of(k * 512, 512), 512)
        total = jnp.zeros((2 * ROWS, 512), F32)
        for n in range(3):
            total += lax.dot_general(grads[n], wv[n, at, :], nt, preferred_element_type=F32)
        dx[:, at] = total.astype(BF16)
        return carry

    lax.fori_loop(0, D // 512, back, 0)


def core(xh, gain, pair, g, w):
    rows = 2 * ROWS
    return pl.pallas_call(
        core_kernel,
        out_shape=(
            jax.ShapeDtypeStruct((rows, HALF), BF16),
            jax.ShapeDtypeStruct((rows, D), BF16),
            jax.ShapeDtypeStruct((rows, 128), F32),
            jax.ShapeDtypeStruct((rows, 128), F32),
        ),
        in_specs=[VMEM, VMEM, VMEM, VMEM, ANY],
        out_specs=(VMEM,) * 4,
        scratch_shapes=[
            pltpu.VMEM((3, D, HALF), BF16),
            pltpu.VMEM((rows, D), BF16),
            pltpu.VMEM((rows, HALF), F32),
            pltpu.VMEM((3, rows, HALF), BF16),
            pltpu.VMEM((3, rows, HALF), BF16),
            DMA((3,)),
        ],
        compiler_params=pltpu.CompilerParams(vmem_limit_bytes=56 * MIB),
        cost_estimate=pl.CostEstimate(flops=26 * 10**9, bytes_accessed=24 * MIB, transcendentals=10**6),
        name="core",
    )(xh, gain, pair, g, w)


def tail_kernel(
    dx, stat, inv, xh, gain, tt, attn,
    inc, attn_o,
    mine, cbuf, pbuf, rdir, rfwd, sbuf, xv, og,
    loc, c_s, c_r, x_s, x_r, st_s, st_r, a_s, a_r, m_s, m_r,
):
    f, x = lax.axis_index("fsdp"), lax.axis_index("tensor")
    c = lax.rem(f, 2)
    mate = f + 1 - 2 * c
    x1, x2, x3 = (lax.rem(x + d, 4) for d in (1, 2, 3))
    low, high = pl.ds(0, ROWS // 2), pl.ds(ROWS // 2, ROWS // 2)

    def cols(j):
        return pl.ds(pl.multiple_of(j * WIDTH, WIDTH), WIDTH)

    rows_own = pl.ds(pl.multiple_of(c * ROWS, ROWS), ROWS)
    rows_mate = pl.ds(pl.multiple_of((1 - c) * ROWS, ROWS), ROWS)
    head_cols = pl.ds(pl.multiple_of(c * HALF, HALF), HALF)
    order = (x2, x1, x3, x)
    load_x = pltpu.make_async_copy(xh.at[c, :, cols(x)], xv, loc.at[0])
    load_x.start()
    keep_a = pltpu.make_async_copy(attn.at[rows_own], attn_o.at[:, head_cols], loc.at[1])
    keep_a.start()
    load_d = []
    for n, j in enumerate(order):
        load_d.append(pltpu.make_async_copy(dx.at[rows_own, cols(j)], mine.at[n], loc.at[2 + n]))
        load_d[-1].start()
    greet()
    sends = []
    for n, j in enumerate(order):
        sends.append(rcopy(dx.at[rows_mate, cols(j)], cbuf.at[n], c_s.at[n], c_r.at[n], fsdp=mate))
    sends.append(rcopy(stat.at[rows_mate], sbuf.at[4], st_s.at[3], st_r.at[4], fsdp=mate))
    sends.append(rcopy(attn.at[rows_mate], attn_o.at[:, head_cols], m_s, m_r, fsdp=mate))

    def summed(n):
        arrived(cbuf.at[n], c_r.at[n])
        load_d[n].wait()
        return mine[n].astype(F32) + cbuf[n].astype(F32)

    pbuf[0] = summed(0).astype(BF16)
    sends.append(rcopy(pbuf.at[0, low], rfwd.at[0], x_s.at[0], x_r.at[0], tensor=x1))
    sends.append(rcopy(pbuf.at[0, high], rfwd.at[1], x_s.at[1], x_r.at[1], tensor=x3))
    pbuf[1] = summed(1).astype(BF16)
    sends.append(rcopy(pbuf.at[1, high], rdir.at[0, high], x_s.at[2], x_r.at[2], tensor=x1))
    pbuf[2] = summed(2).astype(BF16)
    sends.append(rcopy(pbuf.at[2, low], rdir.at[1, low], x_s.at[3], x_r.at[3], tensor=x3))
    arrived(sbuf.at[4], st_r.at[4])
    sbuf[x] = stat[rows_own, :] + sbuf[4]
    for n, to in enumerate((x1, x3, x2)):
        sends.append(rcopy(sbuf.at[x], sbuf.at[x], st_s.at[n], st_r.at[x], tensor=to))
    arrived(rfwd.at[0], x_r.at[0])
    pbuf[1, low, :] = (pbuf[1, low, :].astype(F32) + rfwd[0].astype(F32)).astype(BF16)
    sends.append(rcopy(pbuf.at[1, low], rdir.at[0, low], x_s.at[4], x_r.at[4], tensor=x1))
    arrived(rfwd.at[1], x_r.at[1])
    pbuf[2, high, :] = (pbuf[2, high, :].astype(F32) + rfwd[1].astype(F32)).astype(BF16)
    sends.append(rcopy(pbuf.at[2, high], rdir.at[1, high], x_s.at[5], x_r.at[5], tensor=x3))
    pbuf[3] = summed(3).astype(BF16)
    for frm in (x1, x3, x2):
        arrived(sbuf.at[frm], st_r.at[frm])
    load_x.wait()
    arrived(rdir.at[0, high], x_r.at[2])
    arrived(rdir.at[1, low], x_r.at[3])
    arrived(rdir.at[0, low], x_r.at[4])
    arrived(rdir.at[1, high], x_r.at[5])
    iv = inv[rows_own, 0:1]
    total = (sbuf[0] + sbuf[1] + sbuf[2] + sbuf[3])[:, 0:1]
    coef = iv * iv * total / D
    summed_all = pbuf[3].astype(F32) + rdir[0].astype(F32) + rdir[1].astype(F32)
    grad = iv * (summed_all * gain[:, cols(x)]) - xv[...].astype(F32) * coef
    og[...] = jnp.dot(tt[...], grad.astype(BF16), preferred_element_type=F32).astype(BF16)

    def slot_rows(b):
        return pl.ds(pl.multiple_of(b * CAP, CAP), CAP)

    def a_send(d, carry):
        to = lax.rem(f + d, NF)
        rcopy(og.at[slot_rows(to)], inc.at[slot_rows(f)], a_s.at[to], a_r.at[f], fsdp=to)
        return carry

    lax.fori_loop(1, NF, a_send, 0)
    keep_o = pltpu.make_async_copy(og.at[slot_rows(f)], inc.at[slot_rows(f)], loc.at[6])
    keep_o.start()

    def a_wait(d, carry):
        frm = lax.rem(f + d, NF)
        arrived(inc.at[slot_rows(frm)], a_r.at[frm])
        arrived(og.at[slot_rows(frm)], a_s.at[frm])
        return carry

    lax.fori_loop(1, NF, a_wait, 0)
    keep_o.wait()
    keep_a.wait()
    mate_head = pl.ds(pl.multiple_of((1 - c) * HALF, HALF), HALF)
    arrived(attn_o.at[:, mate_head], m_r)
    for copy in sends:
        copy.wait_send()


def tail(dx, stat, inv, xh, gain, tt, attn):
    block = pltpu.VMEM((4, ROWS, WIDTH), BF16)
    return pl.pallas_call(
        tail_kernel,
        out_shape=(
            jax.ShapeDtypeStruct((SLOTS, WIDTH), BF16),
            jax.ShapeDtypeStruct((ROWS, WIDTH), BF16),
        ),
        in_specs=[ANY, VMEM, VMEM, ANY, VMEM, VMEM, ANY],
        out_specs=(ANY, ANY),
        scratch_shapes=[
            block,
            block,
            block,
            pltpu.VMEM((2, ROWS, WIDTH), BF16),
            pltpu.VMEM((2, ROWS // 2, WIDTH), BF16),
            pltpu.VMEM((5, ROWS, 128), F32),
            pltpu.VMEM((ROWS, WIDTH), BF16),
            pltpu.VMEM((SLOTS, WIDTH), BF16),
            DMA((7,)),
            DMA((4,)), DMA((4,)),
            DMA((6,)), DMA((6,)),
            DMA((4,)), DMA((5,)),
            DMA((NF,)), DMA((NF,)),
            DMA, DMA,
        ],
        compiler_params=pltpu.CompilerParams(
            collective_id=1, has_side_effects=True, vmem_limit_bytes=48 * MIB
        ),
        cost_estimate=pl.CostEstimate(flops=10**9, bytes_accessed=16 * MIB, transcendentals=0),
        name="tail",
    )(dx, stat, inv, xh, gain, tt, attn)


def on_device(item_hidden, item_gain, occ_owner, occ_item, hist_len, user_gain, wqkv, grad_out):
    ids = jnp.stack(
        [occ_owner[:, 0], occ_item, jnp.broadcast_to(hist_len, (ROWS,))]
        + [jnp.zeros((ROWS,), jnp.int32)] * 5
    )
    gain = user_gain.reshape(1, D)
    xh, w, item_embed, wanted, placed, pair, g = front(
        item_hidden, item_gain.reshape(1, WIDTH), wqkv, ids, grad_out
    )
    attn, dx, inv, stat = core(xh.reshape(2 * ROWS, D), gain, pair, g, w)
    incoming, attended = tail(dx, stat, inv, xh, gain, placed, attn)
    item_grads = lax.dot_general(
        wanted, incoming, (((0,), (0,)), ((), ())), preferred_element_type=F32
    )
    return (item_embed, attended, item_grads)


def solution(mesh):
    in_specs = (
        P("fsdp", "tensor"),
        P("tensor"),
        P("fsdp", None),
        P("fsdp"),
        P("fsdp"),
        P(),
        P(None, "fsdp", "tensor"),
        P("fsdp", "tensor"),
    )
    out_specs = (P("fsdp", "tensor"), P("fsdp", "tensor"), P("fsdp", "tensor"))
    return jax.shard_map(
        on_device, mesh=mesh, in_specs=in_specs, out_specs=out_specs, check_vma=False
    )
```

time: 345 us -> 188 us (0.54)
  waiting for transfers between devices: 203 us -> 0 us
  Pallas kernels: 0 us -> 174 us
  matrix products: 47.1 us -> 1.44 us
  starting transfers between devices: 26.8 us -> 0 us
  other arithmetic: 24.2 us -> 0 us
  between operations: 14.6 us -> 1.36 us
  local copies, waits for them, and re-layouts: 19.7 us -> 9.49 us
  blocking collectives: 8.58 us -> 0 us
    pallas_call x0 -> x3, Pallas kernels: none -> 174 us  [the longest x1 91.2 us: front(): pl.pallas_call(front_kernel, out_shape=(jax.ShapeDtypeStruct((2, ROWS, D)...]
    all_gather x2 -> x0, waiting for transfers between devices: 117 us -> none  [the longest x1 92.9 us: on_device(): w_full = lax.all_gather(wqkv, 'fsdp', axis=1, tiled=True)]
    psum x1 -> x0, waiting for transfers between devices: 55.3 us -> none  [on_device(): lax.psum(head_terms.astype(jnp.bfloat16), 'tensor').astype(jnp.float32)]
    dot_general x8 -> x1, matrix products: 43.5 us -> 1.44 us  [on_device(): lax.dot_general(wanted, incoming, (((0,), (0,)), ((), ())), preferred_ele...]
    all_to_all x3 -> x0, waiting for transfers between devices: 29.5 us -> none  [the longest x1 16.9 us: on_device(): lax.all_to_all(found, 'fsdp', split_axis=0, concat_axis=0, tiled=True)]
    all_to_all x3 -> x0, starting transfers between devices: 26.7 us -> none  [the longest x1 9.6 us: on_device(): lax.all_to_all(requests, 'fsdp', split_axis=0, concat_axis=0, tiled=True)]
    reduce_sum x5 -> x0, other arithmetic: 14.9 us -> none  [the longest x1 4.55 us: on_device(): jnp.mean(normed_items.reshape(local_items, ITEM_LEN, width), axis=1)]
    psum x1 -> x0, blocking collectives: 8.58 us -> none  [on_device(): total_sq = lax.psum(partial_sq, 'tensor')]
  transfers between devices with their start and end apart: 6 -> 0, of which waited for: 5 -> 0; matrix products, arithmetic and copies ran while one was open for 5% -> 0% of each run, Pallas kernels for 0% -> 0%
where the time goes in v1:
time: 188 us; the launch traced here: 187 us
  Pallas kernels  174 us (93%)
  local copies, waits for them, and re-layouts  9.49 us (5%)
    pallas_call x1, Pallas kernels, front(): pl.pallas_call(front_kernel, out_shape=(jax.ShapeDtypeStruct((2, ROWS, D)...  91.2 us
    pallas_call x1, Pallas kernels, tail(): pl.pallas_call(tail_kernel, out_shape=(jax.ShapeDtypeStruct((SLOTS, WIDTH...  52 us
    pallas_call x1, Pallas kernels, core(): pl.pallas_call(core_kernel, out_shape=(jax.ShapeDtypeStruct((rows, HALF),...  31 us
    unnamed x20, local copies, waits for them, and re-layouts  8.76 us

profile of v1, /device:TPU:1, one launch (start us, length us, event | category | flops | bytes accessed | tf_op | source)
XLA Modules:
  0.0 186.5 jit_solution(15044844116406504499)
XLA Ops:
  1.3 0.7 stack.11.ids
  2.0 0.0 copy-start
  2.0 1.1 copy-done
  3.2 0.0 copy-start.1
  3.2 1.0 copy-done.1
  4.2 0.0 copy-start.6
  4.2 0.7 copy-done.6
  4.9 91.2 %front.1 = (bf16[2,256,4096]{2,1,0:T(8,128)(2,1)}, bf16[3,4096,512]{2,1,0:T(8,128)(2,1)}, bf16[256,1024]{1,0:T(8,128)(2,1)S(1)}, bf16[512,256]{1,0:T(8,128)(2,1)...) custom-call(bf16[2048,1024]{1,0:T(8,128)(2,1)} %hid.1, ...), custom_call_target="tpu_custom_call" | custom-call | flops 1000000000 | bytes 67108864 | tf_op jit(solution)/shard_map/front/pallas_call | solution.py:303
  96.1 0.0 copy-start.7
  96.1 0.8 copy-done.7
  96.9 0.0 copy-start.8
  96.9 0.6 copy-done.8
  97.5 0.0 copy-start.5
  97.5 31.0 %core.1 = (bf16[512,512]{1,0:T(8,128)(2,1)}, bf16[512,4096]{1,0:T(8,128)(2,1)}, f32[512,128]{1,0:T(8,128)}, f32[512,128]{1,0:T(8,128)}) custom-call(bf16[512,4096]{1,0:T(8,128)(2,1)} %bitcast.12, f32[1,4096]{1,0:T(1,128)} %bitcast.9, s32[2,8,256]{2,1,0:T(8,128)} %copy-done.8, bf16[2,256,512]{2,1,0:T(8,128)(2,1)} %copy-done.7, ...), custom_call_target="tpu_custom_call" | custom-call | flops 25999998976 | bytes 25165824 | tf_op jit(solution)/shard_map/core/pallas_call | solution.py:432
  128.6 0.0 copy-done.5
  128.6 0.0 copy-start.2
  128.6 1.0 copy-done.2
  129.6 0.0 copy-start.3
  129.6 0.9 copy-done.3
  130.6 0.0 copy-start.4
  130.6 0.9 copy-done.4
  131.5 52.0 %tail.1 = (bf16[512,1024]{1,0:T(8,128)(2,1)S(1)}, bf16[256,1024]{1,0:T(8,128)(2,1)S(1)}) custom-call(bf16[512,4096]{1,0:T(8,128)(2,1)} %get-tuple-element.21.dx, f32[512,128]{1,0:T(8,128)S(1)} %copy-done.4, f32[512,128]{1,0:T(8,128)S(1)} %copy-done.3, bf16[2,256,4096]{2,1,0:T(8,128)(2,1)} %get-tuple-element.17.xh, f32[1,4096]{1,0:T(1,128)S(1)} %bitcast.10, ...), custom_call_target="tpu_custom_call" | custom-call | flops 1000000000 | bytes 16777216 | tf_op jit(solution)/shard_map/tail/pallas_call | solution.py:556
  183.5 1.4 fusion
  185.0 0.8 copy.14
  185.7 0.8 copy.15
  (3 shorter events, 0.0 us)
Async XLA Ops:
  2.0 1.1 copy-start
  3.2 1.0 copy-start.1
  4.2 0.7 copy-start.6
  96.1 0.8 copy-start.7
  96.9 0.6 copy-start.8
  97.5 31.1 %copy-start.5 = (f32[4096]{0:T(1024)S(1)}, f32[4096]{0:T(1024)}, u32[]{:S(2)}) copy-start(f32[4096]{0:T(1024)} %param.13) | copy-start | bytes 49156
  128.6 1.0 copy-start.2
  129.6 0.9 copy-start.3
  130.6 0.9 copy-start.4

commit v2 on v0

v2 whole, which is shorter than its diff:
```python
import functools
import math

import jax
import jax.numpy as jnp
from jax import lax
from jax.experimental import pallas as pl
from jax.experimental.pallas import tpu as pltpu
from jax.sharding import PartitionSpec as P

D = 4096
HEAD_DIM = 128
ITEM_LEN = 8
EPSILON = 1e-05
NF = 32
NX = 4
ROWS = 256
CAP = 16
SLOTS = NF * CAP
WIDTH = D // NX
HALF = WIDTH // 2
SHARD = D // NF
GROUP = HALF // 2
TRIO = 3 * GROUP
UNIT = WIDTH // 2
ALL3 = 2 * TRIO
BOTH = 2 * ROWS
F32 = jnp.float32
BF16 = jnp.bfloat16
MIB = 1 << 20


def rcopy(src, dst, send, recv, **where):
    copy = pltpu.make_async_remote_copy(
        src_ref=src,
        dst_ref=dst,
        send_sem=send,
        recv_sem=recv,
        device_id=where,
        device_id_type=pl.DeviceIdType.MESH,
    )
    copy.start()
    return copy


def arrived(ref, sem):
    pltpu.make_async_copy(ref, ref, sem).wait()


def greet():
    f, x = lax.axis_index("fsdp"), lax.axis_index("tensor")
    barrier = pltpu.get_barrier_semaphore()

    def signal(d, carry):
        pl.semaphore_signal(
            barrier,
            inc=1,
            device_id={"fsdp": lax.rem(f + d, NF)},
            device_id_type=pl.DeviceIdType.MESH,
        )
        return carry

    lax.fori_loop(1, NF, signal, 0)
    for d in range(1, NX):
        pl.semaphore_signal(
            barrier,
            inc=1,
            device_id={"tensor": lax.rem(x + d, NX)},
            device_id_type=pl.DeviceIdType.MESH,
        )
    pl.semaphore_wait(barrier, NF - 1 + NX - 1)


def layer_kernel(
    hid, gain, w, ids, g, ugain,
    emb_o, oh_o, attn_o, inc,
    hid_v, idb, sqb, inv_v, tt, fnd, fet, share,
    wv, xh, nrm, acc, qkv, grads, gv, attn, inv_h, stat, sbuf,
    dxs, cbuf, pbuf, rdir, rfwd, og,
    loc, id_s, id_r, sq_s, sq_r, a_s, a_r, w_s, w_r, wm_s, wm_r,
    x_s, x_r, p_s, p_r, g_s, g_r, at_s, at_r, st_s, st_r,
    c_s, c_r, r_s, r_r, b_s, b_r,
):
    f, x = lax.axis_index("fsdp"), lax.axis_index("tensor")
    c = lax.rem(f, 2)
    chip = f // 2
    z, y = lax.rem(chip, 4), chip // 4
    mate = f + 1 - 2 * c
    y1, y2, y3 = (lax.rem(y + d, 4) for d in (1, 2, 3))
    z1, z2, z3 = (lax.rem(z + d, 4) for d in (1, 2, 3))
    x1, x2, x3 = (lax.rem(x + d, 4) for d in (1, 2, 3))
    at_chip = lambda yy, zz: yy * 4 + zz
    yp, ym = at_chip(y1, z) * 2 + c, at_chip(y3, z) * 2 + c
    zp, zm = at_chip(y, z1) * 2 + c, at_chip(y, z3) * 2 + c
    sends = []

    def ds(i, n):
        return pl.ds(pl.multiple_of(i * n, n), n)

    load_hid = pltpu.make_async_copy(hid, hid_v, loc.at[0])
    load_hid.start()
    keep_w = []
    for h in range(2):
        for n in range(3):
            src = w.at[n, :, pl.ds(pl.multiple_of(c * HALF + h * GROUP, GROUP), GROUP)]
            dst = wv.at[ds(f, SHARD), pl.ds(h * TRIO + n * GROUP, GROUP)]
            keep_w.append(pltpu.make_async_copy(src, dst, loc.at[4 + h * 3 + n]))
            keep_w[-1].start()
    keep_id = pltpu.make_async_copy(ids, idb.at[f], loc.at[1])
    keep_id.start()
    keep_g = pltpu.make_async_copy(g.at[:, ds(c, HALF)], gv.at[c], loc.at[2])
    keep_g.start()
    greet()

    def piece(h, s):
        return wv.at[ds(s, SHARD), pl.ds(h * TRIO, TRIO)]

    wcount = [0]

    def wsend(h, s, dev):
        sends.append(rcopy(piece(h, s), piece(h, s), w_s.at[wcount[0]], w_r.at[h * NF + s], fsdp=dev))
        wcount[0] += 1

    def got(h, s):
        arrived(piece(h, s), w_r.at[h * NF + s])

    for h in range(2):
        for n in range(3):
            src = w.at[n, :, pl.ds(pl.multiple_of((1 - c) * HALF + h * GROUP, GROUP), GROUP)]
            dst = wv.at[ds(f, SHARD), pl.ds(h * TRIO + n * GROUP, GROUP)]
            sends.append(rcopy(src, dst, wm_s.at[h * 3 + n], wm_r.at[h * 3 + n], fsdp=mate))
    for h in range(2):
        for copy in keep_w[3 * h : 3 * h + 3]:
            copy.wait()
        for dev in (yp, ym, zp, zm) if h == 0 else (zp, zm, yp, ym):
            wsend(h, f, dev)

    def id_send(d, carry):
        to = lax.rem(f + d, NF)
        rcopy(ids, idb.at[f], id_s.at[to], id_r.at[f], fsdp=to)
        return carry

    lax.fori_loop(1, NF, id_send, 0)
    sends.append(rcopy(g.at[:, ds(1 - c, HALF)], gv.at[c], g_s, g_r, fsdp=mate))

    load_hid.wait()
    lane = lax.broadcasted_iota(jnp.int32, (128, 128), 1)

    def squares(k, total):
        v = hid_v[ds(k, 128), :].astype(F32)
        return jnp.where(lane == k, jnp.sum(v * v, axis=1, keepdims=True), total)

    sqb[x] = lax.fori_loop(0, 16, squares, jnp.zeros((128, 128), F32))
    for n, to in enumerate((x1, x3, x2)):
        sends.append(rcopy(sqb.at[x], sqb.at[x], sq_s.at[n], sq_r.at[x], tensor=to))

    for h in range(2):
        for n in range(3):
            dst = wv.at[ds(mate, SHARD), pl.ds(h * TRIO + n * GROUP, GROUP)]
            arrived(dst, wm_r.at[h * 3 + n])
        for dev in (yp, ym, zp, zm) if h == 0 else (zp, zm, yp, ym):
            wsend(h, mate, dev)

    def id_wait(d, carry):
        frm = lax.rem(f + d, NF)
        arrived(idb.at[frm], id_r.at[frm])
        return carry

    lax.fori_loop(1, NF, id_wait, 0)
    keep_id.wait()
    row = lax.broadcasted_iota(jnp.int32, (SLOTS, ROWS), 0)
    col = lax.broadcasted_iota(jnp.int32, (SLOTS, ROWS), 1)
    slot = lax.rem(row, CAP).astype(F32)
    group = row // CAP
    t_at = lax.broadcasted_iota(jnp.int32, (ROWS, ROWS), 0)
    s_at = lax.broadcasted_iota(jnp.int32, (ROWS, ROWS), 1)
    before = (t_at < s_at).astype(F32).astype(BF16)

    def slots_of(named):
        rank = jnp.dot(named.astype(F32).astype(BF16), before, preferred_element_type=F32)
        return named & (rank == slot)

    mine_owner = jnp.broadcast_to(idb[f, 0:1, :], (SLOTS, ROWS))
    tt[...] = slots_of(mine_owner == group).astype(F32).astype(BF16)
    table = idb[...].reshape(NF * 8, ROWS).astype(F32).astype(BF16)
    pick_owner = (col == group * 8).astype(F32).astype(BF16)
    pick_item = (col == group * 8 + 1).astype(F32).astype(BF16)
    owner_all = jnp.dot(pick_owner, table, preferred_element_type=F32)
    item_all = jnp.dot(pick_item, table, preferred_element_type=F32)
    taken = slots_of(owner_all == f.astype(F32))
    wanted = jnp.sum(jnp.where(taken, item_all + 1.0, 0.0), axis=1, keepdims=True) - 1.0
    oh_o[...] = (wanted == col.astype(F32)).astype(F32).astype(BF16)

    for frm in (x1, x3, x2):
        arrived(sqb.at[frm], sq_r.at[frm])
    inv_v[...] = lax.rsqrt((sqb[0] + sqb[1] + sqb[2] + sqb[3]) / D + EPSILON)

    def pool(k, carry):
        v = hid_v[ds(k, 128), :].astype(F32)
        inv = jnp.sum(jnp.where(lane == k, inv_v[...], 0.0), axis=1, keepdims=True)
        total = jnp.sum((v * inv).reshape(16, ITEM_LEN, WIDTH), axis=1)
        emb_o[ds(k, 16), :] = (total * (1.0 / ITEM_LEN) * gain[...]).astype(BF16)
        return carry

    lax.fori_loop(0, 16, pool, 0)
    fnd[...] = jnp.dot(oh_o[...], emb_o[...], preferred_element_type=F32).astype(BF16)

    def a_send(d, carry):
        to = lax.rem(f + d, NF)
        rcopy(fnd.at[ds(to, CAP)], fet.at[ds(f, CAP)], a_s.at[to], a_r.at[f], fsdp=to)
        return carry

    lax.fori_loop(1, NF, a_send, 0)
    fet[ds(f, CAP), :] = fnd[ds(f, CAP), :]

    prev = (at_chip(y3, z), at_chip(y, z3))
    nxt = (at_chip(y1, z), at_chip(y, z1))
    far = (at_chip(y2, z), at_chip(y, z2))
    ways = ((yp, ym), (zp, zm))
    for h in range(2):
        up, dn = ways[h]
        got(h, prev[h] * 2)
        wsend(h, prev[h] * 2, up)
        got(h, nxt[h] * 2 + 1)
        wsend(h, nxt[h] * 2 + 1, dn)
    for h in range(2):
        got(h, prev[h] * 2 + 1)
        got(h, nxt[h] * 2)
        for s in (prev[h] * 2, nxt[h] * 2 + 1, prev[h] * 2 + 1, nxt[h] * 2):
            for dev in ways[1 - h]:
                wsend(h, s, dev)
    for h in range(2):
        for r in range(2):
            got(h, far[h] * 2 + r)
            for dev in ways[1 - h]:
                wsend(h, far[h] * 2 + r, dev)

    def a_wait(d, carry):
        frm = lax.rem(f + d, NF)
        arrived(fet.at[ds(frm, CAP)], a_r.at[frm])
        return carry

    lax.fori_loop(1, NF, a_wait, 0)
    share[...] = lax.dot_general(
        tt[...], fet[...], (((0,), (0,)), ((), ())), preferred_element_type=F32
    ).astype(BF16)

    def xpart(j, h):
        return xh.at[c, pl.ds(h * (ROWS // 2), ROWS // 2), ds(j, WIDTH)]

    def xwhole(k, j):
        return xh.at[k, :, ds(j, WIDTH)]

    keep_x = pltpu.make_async_copy(share, xwhole(c, x), loc.at[3])
    keep_x.start()
    for h in range(2):
        half = share.at[pl.ds(h * (ROWS // 2), ROWS // 2)]
        sends.append(rcopy(half, xpart(x, h), x_s.at[h], x_r.at[2 * x + h], tensor=x1))
        sends.append(rcopy(half, xpart(x, h), x_s.at[2 + h], x_r.at[2 * x + h], tensor=x3))
    sends.append(rcopy(share, xwhole(c, x), p_s.at[0], p_r.at[x], fsdp=mate))

    def third(n):
        yy, zz = ((y, z), (y3, z3), (y1, z1), (y2, z2))[n]
        from_low = (at_chip(yy, z3), at_chip(y3, zz))
        from_high = (at_chip(yy, z1), at_chip(y1, zz))
        for h in range(2):
            up, dn = ways[1 - h]
            got(h, from_low[h] * 2)
            wsend(h, from_low[h] * 2, up)
            got(h, from_high[h] * 2 + 1)
            wsend(h, from_high[h] * 2 + 1, dn)
        for h in range(2):
            got(h, from_low[h] * 2 + 1)
            got(h, from_high[h] * 2)

    def x_forward():
        for h, (frm, to) in enumerate(((x3, x1), (x1, x3))):
            arrived(xpart(frm, h), x_r.at[2 * frm + h])
            sends.append(rcopy(xpart(frm, h), xpart(frm, h), x_s.at[4 + h], x_r.at[2 * frm + h], tensor=to))
        for h, frm in enumerate((x3, x1)):
            arrived(xpart(frm, 1 - h), x_r.at[2 * frm + 1 - h])
            sends.append(rcopy(xwhole(c, frm), xwhole(c, frm), p_s.at[1 + h], p_r.at[frm], fsdp=mate))

    def x_finish():
        for h in range(2):
            arrived(xpart(x2, h), x_r.at[2 * x2 + h])
        sends.append(rcopy(xwhole(c, x2), xwhole(c, x2), p_s.at[3], p_r.at[x2], fsdp=mate))
        keep_x.wait()

    def norm(k, carry):
        h, m = k // 8, lax.rem(k, 8)
        v = xh[h, ds(m, 32), :].astype(F32)
        inv = lax.rsqrt(jnp.sum(v * v, axis=1, keepdims=True) / D + EPSILON)
        nrm[ds(k, 32), :] = (v * inv * ugain[...]).astype(BF16)
        inv_h[ds(k, 32), :] = jnp.broadcast_to(inv, (32, 128))
        return carry

    third(0)
    x_forward()
    third(1)
    third(2)
    x_finish()
    lax.fori_loop(c * 8, c * 8 + 8, norm, 0)
    third(3)
    for j in (x, x3, x1, x2):
        arrived(xwhole(1 - c, j), p_r.at[j])
    lax.fori_loop((1 - c) * 8, (1 - c) * 8 + 8, norm, 0)

    def project(h, k, depth):
        acc[h] += jnp.dot(
            nrm[:, ds(k, depth)],
            wv[ds(k, depth), h * TRIO : (h + 1) * TRIO],
            preferred_element_type=F32,
        )

    def near_h1(t, carry):
        project(1, lax.rem(y + 3 + t, 4), 1024)
        return carry

    def near_h0(t, carry):
        project(0, at_chip(lax.rem(t, 4), lax.rem(z + 3 + t // 4, 4)), 256)
        return carry

    def far_h0(t, carry):
        project(0, at_chip(t, z2), 256)
        return carry

    acc[...] = jnp.zeros_like(acc)
    lax.fori_loop(0, 3, near_h1, 0)
    lax.fori_loop(0, 12, near_h0, 0)
    for yy in (y, y3, y1, y2):
        for r in range(2):
            got(0, at_chip(yy, z2) * 2 + r)
    lax.fori_loop(0, 4, far_h0, 0)
    qkv[:, 0:TRIO] = acc[0].astype(BF16)
    for zz in (z, z3, z1, z2):
        for r in range(2):
            got(1, at_chip(y2, zz) * 2 + r)
    project(1, y2, 1024)
    qkv[:, TRIO:ALL3] = acc[1].astype(BF16)

    factor = 1.0 / math.sqrt(HEAD_DIM)
    t_row = lax.broadcasted_iota(jnp.int32, (ROWS, HEAD_DIM), 0)
    nt = (((1,), (1,)), ((), ()))
    tn = (((0,), (0,)), ((), ()))
    keep_g.wait()
    arrived(gv.at[1 - c], g_r)

    def attend(k, carry):
        h, n = k // 4, lax.rem(k, 4)
        rows = ds(h, ROWS)
        cols = ds(n, HEAD_DIM)
        base = (n // 2) * TRIO + lax.rem(n, 2) * HEAD_DIM
        q_at, k_at, v_at = (
            pl.ds(pl.multiple_of(base + i * GROUP, HEAD_DIM), HEAD_DIM) for i in range(3)
        )
        length = idb[chip * 2 + h, 2:3, :]
        allowed = (s_at <= t_at) & (s_at < length)
        live = t_row < length[:, :HEAD_DIM]
        qq, kk, vv = qkv[rows, q_at], qkv[rows, k_at], qkv[rows, v_at]
        gg = jnp.where(live, gv[h, :, cols].astype(F32), 0.0).astype(BF16)
        scores = lax.dot_general(qq, kk, nt, preferred_element_type=F32) * factor
        scores = jnp.where(allowed, scores, -1e30)
        top = jnp.max(scores, axis=1, keepdims=True)
        raised = jnp.where(allowed, jnp.exp(scores - top), 0.0)
        probs = raised * (1.0 / jnp.sum(raised, axis=1, keepdims=True))
        pb = probs.astype(BF16)
        out = jnp.dot(pb, vv, preferred_element_type=F32)
        attn[rows, cols] = jnp.where(live, out, 0.0).astype(BF16)
        dv = lax.dot_general(pb, gg, tn, preferred_element_type=F32).astype(BF16)
        dp = lax.dot_general(gg, vv, nt, preferred_element_type=F32)
        mid = jnp.sum(probs * dp, axis=1, keepdims=True)
        dsc = (probs * (dp - mid) * factor).astype(BF16)
        dq = jnp.dot(dsc, kk, preferred_element_type=F32).astype(BF16)
        dk = lax.dot_general(dsc, qq, tn, preferred_element_type=F32).astype(BF16)
        grads[rows, q_at] = dq
        grads[rows, k_at] = dk
        grads[rows, v_at] = dv
        terms = (
            dq.astype(F32) * qq.astype(F32)
            + dk.astype(F32) * kk.astype(F32)
            + dv.astype(F32) * vv.astype(F32)
        )
        stat[rows, :] += jnp.broadcast_to(jnp.sum(terms, axis=1, keepdims=True), (ROWS, 128))
        return carry

    stat[...] = jnp.zeros_like(stat)
    lax.fori_loop(0, 8, attend, 0)

    rows_own, rows_mate = ds(c, ROWS), ds(1 - c, ROWS)
    low, high = pl.ds(0, ROWS // 2), pl.ds(ROWS // 2, ROWS // 2)
    sends.append(rcopy(stat.at[rows_mate], sbuf.at[4], st_s.at[3], st_r.at[4], fsdp=mate))
    order = (x2, x1, x3, x)

    def back(u):
        q, n = u // 4, u % 4
        at = pl.ds(pl.multiple_of(order[n] * WIDTH + q * UNIT, UNIT), UNIT)
        dxs[u] = lax.dot_general(grads[...], wv[at, :], nt, preferred_element_type=F32).astype(BF16)
        sends.append(rcopy(dxs.at[u, rows_mate], cbuf.at[u], c_s.at[u], c_r.at[u], fsdp=mate))

    def summed(u):
        arrived(cbuf.at[u], c_r.at[u])
        pbuf[u] = (dxs[u, rows_own, :].astype(F32) + cbuf[u].astype(F32)).astype(BF16)

    def ring(q, k, src, dst, to):
        sends.append(rcopy(src, dst, r_s.at[q * 6 + k], r_r.at[q * 6 + k], tensor=to))

    def far_out(q):
        summed(q * 4)
        ring(q, 0, pbuf.at[q * 4, low], rfwd.at[q, 0], x1)
        ring(q, 1, pbuf.at[q * 4, high], rfwd.at[q, 1], x3)

    def near_out(q):
        summed(q * 4 + 1)
        ring(q, 2, pbuf.at[q * 4 + 1, high], rdir.at[q, 0, high], x1)
        summed(q * 4 + 2)
        ring(q, 3, pbuf.at[q * 4 + 2, low], rdir.at[q, 1, low], x3)

    def add_out(q):
        arrived(rfwd.at[q, 0], r_r.at[q * 6])
        u = q * 4 + 1
        pbuf[u, low, :] = (pbuf[u, low, :].astype(F32) + rfwd[q, 0].astype(F32)).astype(BF16)
        ring(q, 4, pbuf.at[u, low], rdir.at[q, 0, low], x1)
        arrived(rfwd.at[q, 1], r_r.at[q * 6 + 1])
        u = q * 4 + 2
        pbuf[u, high, :] = (pbuf[u, high, :].astype(F32) + rfwd[q, 1].astype(F32)).astype(BF16)
        ring(q, 5, pbuf.at[u, high], rdir.at[q, 1, high], x3)

    def a_out(q):
        arrived(rdir.at[q, 0, high], r_r.at[q * 6 + 2])
        arrived(rdir.at[q, 1, low], r_r.at[q * 6 + 3])
        arrived(rdir.at[q, 0, low], r_r.at[q * 6 + 4])
        arrived(rdir.at[q, 1, high], r_r.at[q * 6 + 5])
        iv = inv_h[rows_own, 0:1]
        total = (sbuf[0] + sbuf[1] + sbuf[2] + sbuf[3])[:, 0:1]
        coef = iv * iv * total / D
        at = pl.ds(pl.multiple_of(x * WIDTH + q * UNIT, UNIT), UNIT)
        parts = pbuf[q * 4 + 3].astype(F32) + rdir[q, 0].astype(F32) + rdir[q, 1].astype(F32)
        grad = iv * (parts * ugain[:, at]) - xh[c, :, at].astype(F32) * coef
        og[q] = jnp.dot(tt[...], grad.astype(BF16), preferred_element_type=F32).astype(BF16)

        def send(d, carry):
            to = lax.rem(f + d, NF)
            here, there = og.at[q, ds(to, CAP)], inc.at[ds(f, CAP), pl.ds(q * UNIT, UNIT)]
            rcopy(here, there, b_s.at[q * NF + to], b_r.at[q * NF + f], fsdp=to)
            return carry

        lax.fori_loop(1, NF, send, 0)
        keep = pltpu.make_async_copy(
            og.at[q, ds(f, CAP)], inc.at[ds(f, CAP), pl.ds(q * UNIT, UNIT)], loc.at[10 + q]
        )
        keep.start()
        return keep

    back(0)
    back(1)
    far_out(0)
    back(2)
    arrived(sbuf.at[4], st_r.at[4])
    sbuf[x] = stat[rows_own, :] + sbuf[4]
    for n, to in enumerate((x1, x3, x2)):
        sends.append(rcopy(sbuf.at[x], sbuf.at[x], st_s.at[n], st_r.at[x], tensor=to))
    near_out(0)
    keep_a = pltpu.make_async_copy(attn.at[rows_own], attn_o.at[:, ds(c, HALF)], loc.at[12])
    keep_a.start()
    sends.append(rcopy(attn.at[rows_mate], attn_o.at[:, ds(c, HALF)], at_s, at_r, fsdp=mate))
    back(3)
    back(4)
    back(5)
    back(6)
    add_out(0)
    far_out(1)
    near_out(1)
    back(7)
    summed(3)
    summed(7)
    for frm in (x1, x3, x2):
        arrived(sbuf.at[frm], st_r.at[frm])
    add_out(1)
    keeps = [a_out(0)]
    keeps.append(a_out(1))

    def finish(d, carry):
        frm = lax.rem(f + d, NF)
        for q in range(2):
            block = inc.at[ds(frm, CAP), pl.ds(q * UNIT, UNIT)]
            arrived(block, b_r.at[q * NF + frm])
            arrived(og.at[q, ds(frm, CAP)], b_s.at[q * NF + frm])
        arrived(ids, id_s.at[frm])
        arrived(fnd.at[ds(frm, CAP)], a_s.at[frm])
        return carry

    lax.fori_loop(1, NF, finish, 0)
    arrived(attn_o.at[:, ds(1 - c, HALF)], at_r)
    for copy in keeps:
        copy.wait()
    keep_a.wait()
    for copy in sends:
        copy.wait_send()


ANY = pl.BlockSpec(memory_space=pl.ANY)
VMEM = pl.BlockSpec(memory_space=pltpu.VMEM)
DMA = pltpu.SemaphoreType.DMA


def layer(item_hidden, item_gain, wqkv, ids, grad_out, user_gain):
    vm = pltpu.VMEM
    return pl.pallas_call(
        layer_kernel,
        out_shape=(
            jax.ShapeDtypeStruct((ROWS, WIDTH), BF16),
            jax.ShapeDtypeStruct((SLOTS, ROWS), BF16),
            jax.ShapeDtypeStruct((ROWS, WIDTH), BF16),
            jax.ShapeDtypeStruct((SLOTS, WIDTH), BF16),
        ),
        in_specs=[ANY, VMEM, ANY, ANY, ANY, VMEM],
        out_specs=(VMEM, VMEM, ANY, ANY),
        scratch_shapes=[
            vm((ROWS * ITEM_LEN, WIDTH), BF16),
            vm((NF, 8, ROWS), jnp.int32),
            vm((NX, 128, 128), F32),
            vm((128, 128), F32),
            vm((SLOTS, ROWS), BF16),
            vm((SLOTS, WIDTH), BF16),
            vm((SLOTS, WIDTH), BF16),
            vm((ROWS, WIDTH), BF16),
            vm((D, ALL3), BF16),
            vm((2, ROWS, D), BF16),
            vm((BOTH, D), BF16),
            vm((2, BOTH, TRIO), F32),
            vm((BOTH, ALL3), BF16),
            vm((BOTH, ALL3), BF16),
            vm((2, ROWS, HALF), BF16),
            vm((BOTH, HALF), BF16),
            vm((BOTH, 128), F32),
            vm((BOTH, 128), F32),
            vm((5, ROWS, 128), F32),
            vm((8, BOTH, UNIT), BF16),
            vm((8, ROWS, UNIT), BF16),
            vm((8, ROWS, UNIT), BF16),
            vm((2, 2, ROWS, UNIT), BF16),
            vm((2, 2, ROWS // 2, UNIT), BF16),
            vm((2, SLOTS, UNIT), BF16),
            DMA((13,)),
            DMA((NF,)), DMA((NF,)),
            DMA((3,)), DMA((NX,)),
            DMA((NF,)), DMA((NF,)),
            DMA((64,)), DMA((2 * NF,)),
            DMA((6,)), DMA((6,)),
            DMA((6,)), DMA((2 * NX,)),
            DMA((4,)), DMA((NX,)),
            DMA, DMA,
            DMA, DMA,
            DMA((4,)), DMA((5,)),
            DMA((8,)), DMA((8,)),
            DMA((12,)), DMA((12,)),
            DMA((2 * NF,)), DMA((2 * NF,)),
        ],
        compiler_params=pltpu.CompilerParams(
            collective_id=0, has_side_effects=True, vmem_limit_bytes=62 * MIB
        ),
        cost_estimate=pl.CostEstimate(flops=27 * 10**9, bytes_accessed=64 * MIB, transcendentals=10**6),
        name="layer",
    )(item_hidden, item_gain, wqkv, ids, grad_out, user_gain)


def on_device(item_hidden, item_gain, occ_owner, occ_item, hist_len, user_gain, wqkv, grad_out):
    ids = jnp.stack(
        [occ_owner[:, 0], occ_item, jnp.broadcast_to(hist_len, (ROWS,))]
        + [jnp.zeros((ROWS,), jnp.int32)] * 5
    )
    item_embed, wanted, attended, incoming = layer(
        item_hidden, item_gain.reshape(1, WIDTH), wqkv, ids, grad_out, user_gain.reshape(1, D)
    )
    item_grads = lax.dot_general(
        wanted, incoming, (((0,), (0,)), ((), ())), preferred_element_type=F32
    )
    return (item_embed, attended, item_grads)


def solution(mesh):
    in_specs = (
        P("fsdp", "tensor"),
        P("tensor"),
        P("fsdp", None),
        P("fsdp"),
        P("fsdp"),
        P(),
        P(None, "fsdp", "tensor"),
        P("fsdp", "tensor"),
    )
    out_specs = (P("fsdp", "tensor"), P("fsdp", "tensor"), P("fsdp", "tensor"))
    return jax.shard_map(
        on_device, mesh=mesh, in_specs=in_specs, out_specs=out_specs, check_vma=False
    )
```

time: 345 us -> 155 us (0.45)
  waiting for transfers between devices: 203 us -> 0 us
  Pallas kernels: 0 us -> 145 us
  matrix products: 47.1 us -> 2.76 us
  starting transfers between devices: 26.8 us -> 0 us
  other arithmetic: 24.2 us -> 0 us
  local copies, waits for them, and re-layouts: 19.7 us -> 5.05 us
  between operations: 14.6 us -> 1.31 us
  blocking collectives: 8.58 us -> 0 us
    pallas_call x0 -> x1, Pallas kernels: none -> 145 us  [layer(): pl.pallas_call(layer_kernel, out_shape=(jax.ShapeDtypeStruct((ROWS, WIDTH...]
    all_gather x2 -> x0, waiting for transfers between devices: 117 us -> none  [the longest x1 92.9 us: on_device(): w_full = lax.all_gather(wqkv, 'fsdp', axis=1, tiled=True)]
    psum x1 -> x0, waiting for transfers between devices: 55.3 us -> none  [on_device(): lax.psum(head_terms.astype(jnp.bfloat16), 'tensor').astype(jnp.float32)]
    dot_general x8 -> x1, matrix products: 43.5 us -> 2.76 us  [on_device(): lax.dot_general(wanted, incoming, (((0,), (0,)), ((), ())), preferred_ele...]
    all_to_all x3 -> x0, waiting for transfers between devices: 29.5 us -> none  [the longest x1 16.9 us: on_device(): lax.all_to_all(found, 'fsdp', split_axis=0, concat_axis=0, tiled=True)]
    all_to_all x3 -> x0, starting transfers between devices: 26.7 us -> none  [the longest x1 9.6 us: on_device(): lax.all_to_all(requests, 'fsdp', split_axis=0, concat_axis=0, tiled=True)]
    reduce_sum x5 -> x0, other arithmetic: 14.9 us -> none  [the longest x1 4.55 us: on_device(): jnp.mean(normed_items.reshape(local_items, ITEM_LEN, width), axis=1)]
    psum x1 -> x0, blocking collectives: 8.58 us -> none  [on_device(): total_sq = lax.psum(partial_sq, 'tensor')]
  transfers between devices with their start and end apart: 6 -> 0, of which waited for: 5 -> 0; matrix products, arithmetic and copies ran while one was open for 5% -> 0% of each run, Pallas kernels for 0% -> 0%
where the time goes in v2:
time: 155 us; the launch traced here: 154 us
  Pallas kernels  145 us (94%)
  local copies, waits for them, and re-layouts  5.05 us (3%)
  matrix products  2.76 us (2%)
    pallas_call x1, Pallas kernels, layer(): pl.pallas_call(layer_kernel, out_shape=(jax.ShapeDtypeStruct((ROWS, WIDTH...  145 us
    unnamed x2, local copies, waits for them, and re-layouts  3.73 us

profile of v2, /device:TPU:1, one launch (start us, length us, event | category | flops | bytes accessed | tf_op | source)
XLA Modules:
  0.0 154.5 jit_solution(5521274209001088054)
XLA Ops:
  1.3 1.3 stack.11.ids
  2.6 145.4 %layer.1 = (bf16[256,1024]{1,0:T(8,128)(2,1)}, bf16[512,256]{1,0:T(8,128)(2,1)}, bf16[256,1024]{1,0:T(8,128)(2,1)}, bf16[512,1024]{1,0:T(8,128)(2,1)}) custom-call(bf16[2048,1024]{1,0:T(8,128)(2,1)} %hid.1, f32[1,1024]{1,0:T(1,128)} %bitcast.11, bf16[3,128,1024]{2,1,0:T(8,128)(2,1)} %w.1, s32[8,256]{1,0:T(8,128)} %stack.11.ids, bf16[256,1024]{1,0:T(8,128)(2,1)} %g.1, ...), custom_call_target="tpu_custom_call" | custom-call | flops 27000000512 | bytes 67108864 | tf_op jit(solution)/shard_map/layer/pallas_call | solution.py:509
  148.0 2.8 %fusion = f32[256,1024]{1,0:T(8,128)} fusion(bf16[512,256]{1,0:T(8,128)(2,1)} %get-tuple-element.9, bf16[512,1024]{1,0:T(8,128)(2,1)} %get-tuple-element.10), kind=kOutput, calls=%fused_computation | convolution fusion | flops 268435456 | bytes 2359296 | tf_op jit(solution)/shard_map/dot_general | solution.py:576
  150.7 1.9 %copy.14 = bf16[256,1024]{1,0:T(8,128)(2,1)} copy(bf16[256,1024]{1,0:T(8,128)(2,1)} %get-tuple-element.14) | data formatting | bytes 1048576
  152.6 1.9 %copy.15 = bf16[256,1024]{1,0:T(8,128)(2,1)} copy(bf16[256,1024]{1,0:T(8,128)(2,1)} %get-tuple-element.15) | data formatting | bytes 1048576
  (3 shorter events, 0.0 us)

commit v3 on v2

--- a/solution.py
+++ b/solution.py
@@ -22,7 +22,9 @@
 SHARD = D // NF
 GROUP = HALF // 2
 TRIO = 3 * GROUP
-UNIT = WIDTH // 2
+PIECES = 4
+UNIT = WIDTH // PIECES
+PEERS = NF - 1
 ALL3 = 2 * TRIO
 BOTH = 2 * ROWS
 F32 = jnp.float32
@@ -68,14 +70,17 @@
             device_id={"tensor": lax.rem(x + d, NX)},
             device_id_type=pl.DeviceIdType.MESH,
         )
-    pl.semaphore_wait(barrier, NF - 1 + NX - 1)
+
+
+def greeted():
+    pl.semaphore_wait(pltpu.get_barrier_semaphore(), NF - 1 + NX - 1)
 
 
 def layer_kernel(
     hid, gain, w, ids, g, ugain,
     emb_o, oh_o, attn_o, inc,
     hid_v, idb, sqb, inv_v, tt, fnd, fet, share,
-    wv, xh, nrm, acc, qkv, grads, gv, attn, inv_h, stat, sbuf,
+    wv, xh, nrm, acc, qkv, grads, gv, attn, inv_h, stat, sbuf, srow,
     dxs, cbuf, pbuf, rdir, rfwd, og,
     loc, id_s, id_r, sq_s, sq_r, a_s, a_r, w_s, w_r, wm_s, wm_r,
     x_s, x_r, p_s, p_r, g_s, g_r, at_s, at_r, st_s, st_r,
@@ -112,61 +117,110 @@
     keep_g.start()
     greet()
 
+    load_hid.wait()
+    lane = lax.broadcasted_iota(jnp.int32, (128, 128), 1)
+
+    def squares(k, total):
+        v = hid_v[ds(k, 128), :].astype(F32)
+        return jnp.where(lane == k, jnp.sum(v * v, axis=1, keepdims=True), total)
+
+    sqb[x] = lax.fori_loop(0, 16, squares, jnp.zeros((128, 128), F32))
+    greeted()
+
     def piece(h, s):
         return wv.at[ds(s, SHARD), pl.ds(h * TRIO, TRIO)]
 
+    def part(h, s, k):
+        at = pl.multiple_of(s * SHARD + k * (SHARD // 2), SHARD // 2)
+        return wv.at[pl.ds(at, SHARD // 2), pl.ds(h * TRIO, TRIO)]
+
     wcount = [0]
 
-    def wsend(h, s, dev):
-        sends.append(rcopy(piece(h, s), piece(h, s), w_s.at[wcount[0]], w_r.at[h * NF + s], fsdp=dev))
+    def wsend(ref, sem, dev):
+        sends.append(rcopy(ref, ref, w_s.at[wcount[0]], w_r.at[sem], fsdp=dev))
         wcount[0] += 1
 
+    def full(h, s, devs):
+        for dev in devs:
+            wsend(piece(h, s), (h * NF + s) * 2, dev)
+
+    def half(h, s, k, dev):
+        wsend(part(h, s, k), (h * NF + s) * 2 + k, dev)
+
     def got(h, s):
-        arrived(piece(h, s), w_r.at[h * NF + s])
+        arrived(piece(h, s), w_r.at[(h * NF + s) * 2])
+
+    def got_halves(h, s):
+        for k in range(2):
+            arrived(part(h, s, k), w_r.at[(h * NF + s) * 2 + k])
+
+    ways = ((yp, ym), (zp, zm))
+    prev = (at_chip(y3, z) * 2, at_chip(y, z3) * 2 + 1)
+    nxt = (at_chip(y1, z) * 2, at_chip(y, z1) * 2 + 1)
+    far = (at_chip(y2, z) * 2, at_chip(y, z2) * 2 + 1)
+    own = (chip * 2, chip * 2 + 1)
 
     for h in range(2):
         for n in range(3):
             src = w.at[n, :, pl.ds(pl.multiple_of((1 - c) * HALF + h * GROUP, GROUP), GROUP)]
             dst = wv.at[ds(f, SHARD), pl.ds(h * TRIO + n * GROUP, GROUP)]
             sends.append(rcopy(src, dst, wm_s.at[h * 3 + n], wm_r.at[h * 3 + n], fsdp=mate))
+    first = (lax.select(c == 0, yp, zp), lax.select(c == 0, ym, zm))
+    second = (lax.select(c == 0, zp, yp), lax.select(c == 0, zm, ym))
     for h in range(2):
         for copy in keep_w[3 * h : 3 * h + 3]:
             copy.wait()
-        for dev in (yp, ym, zp, zm) if h == 0 else (zp, zm, yp, ym):
-            wsend(h, f, dev)
+        full(h, f, first)
+        full(h, f, second)
+    for n, to in enumerate((x1, x3, x2)):
+        sends.append(rcopy(sqb.at[x], sqb.at[x], sq_s.at[n], sq_r.at[x], tensor=to))
 
     def id_send(d, carry):
-        to = lax.rem(f + d, NF)
-        rcopy(ids, idb.at[f], id_s.at[to], id_r.at[f], fsdp=to)
+        rcopy(ids, idb.at[f], id_s, id_r, fsdp=lax.rem(f + d, NF))
         return carry
 
     lax.fori_loop(1, NF, id_send, 0)
     sends.append(rcopy(g.at[:, ds(1 - c, HALF)], gv.at[c], g_s, g_r, fsdp=mate))
-
-    load_hid.wait()
-    lane = lax.broadcasted_iota(jnp.int32, (128, 128), 1)
-
-    def squares(k, total):
-        v = hid_v[ds(k, 128), :].astype(F32)
-        return jnp.where(lane == k, jnp.sum(v * v, axis=1, keepdims=True), total)
-
-    sqb[x] = lax.fori_loop(0, 16, squares, jnp.zeros((128, 128), F32))
-    for n, to in enumerate((x1, x3, x2)):
-        sends.append(rcopy(sqb.at[x], sqb.at[x], sq_s.at[n], sq_r.at[x], tensor=to))
 
     for h in range(2):
         for n in range(3):
             dst = wv.at[ds(mate, SHARD), pl.ds(h * TRIO + n * GROUP, GROUP)]
             arrived(dst, wm_r.at[h * 3 + n])
-        for dev in (yp, ym, zp, zm) if h == 0 else (zp, zm, yp, ym):
-            wsend(h, mate, dev)
-
-    def id_wait(d, carry):
-        frm = lax.rem(f + d, NF)
-        arrived(idb.at[frm], id_r.at[frm])
-        return carry
-
-    lax.fori_loop(1, NF, id_wait, 0)
+        full(h, mate, second)
+        full(h, mate, first)
+
+    def second_near(h):
+        for r in range(2):
+            got(h, prev[r])
+            half(h, prev[r], 0, ways[r][0])
+            got(h, nxt[r])
+            half(h, nxt[r], 1, ways[r][1])
+        for r in range(2):
+            full(h, prev[r], ways[1 - r])
+            full(h, nxt[r], ways[1 - r])
+
+    def second_far(h):
+        for r in range(2):
+            got_halves(h, far[r])
+            full(h, far[r], ways[1 - r])
+
+    def third(h, n):
+        yy, zz = ((y, z), (y3, z3), (y1, z1), (y2, z2))[n]
+        low = (at_chip(yy, z3) * 2, at_chip(y3, zz) * 2 + 1)
+        high = (at_chip(yy, z1) * 2, at_chip(y1, zz) * 2 + 1)
+        for r in range(2):
+            got(h, low[r])
+            half(h, low[r], 0, ways[1 - r][0])
+            got(h, high[r])
+            half(h, high[r], 1, ways[1 - r][1])
+
+    def last(h, which):
+        for n in which:
+            yy, zz = ((y, z), (y3, z3), (y1, z1), (y2, z2))[n]
+            got_halves(h, at_chip(yy, z2) * 2)
+            got_halves(h, at_chip(y2, zz) * 2 + 1)
+
+    arrived(idb.at[pl.ds(0, PEERS)], id_r)
     keep_id.wait()
     row = lax.broadcasted_iota(jnp.int32, (SLOTS, ROWS), 0)
     col = lax.broadcasted_iota(jnp.int32, (SLOTS, ROWS), 1)
@@ -207,40 +261,15 @@
 
     def a_send(d, carry):
         to = lax.rem(f + d, NF)
-        rcopy(fnd.at[ds(to, CAP)], fet.at[ds(f, CAP)], a_s.at[to], a_r.at[f], fsdp=to)
+        rcopy(fnd.at[ds(to, CAP)], fet.at[ds(f, CAP)], a_s, a_r, fsdp=to)
         return carry
 
     lax.fori_loop(1, NF, a_send, 0)
     fet[ds(f, CAP), :] = fnd[ds(f, CAP), :]
-
-    prev = (at_chip(y3, z), at_chip(y, z3))
-    nxt = (at_chip(y1, z), at_chip(y, z1))
-    far = (at_chip(y2, z), at_chip(y, z2))
-    ways = ((yp, ym), (zp, zm))
-    for h in range(2):
-        up, dn = ways[h]
-        got(h, prev[h] * 2)
-        wsend(h, prev[h] * 2, up)
-        got(h, nxt[h] * 2 + 1)
-        wsend(h, nxt[h] * 2 + 1, dn)
-    for h in range(2):
-        got(h, prev[h] * 2 + 1)
-        got(h, nxt[h] * 2)
-        for s in (prev[h] * 2, nxt[h] * 2 + 1, prev[h] * 2 + 1, nxt[h] * 2):
-            for dev in ways[1 - h]:
-                wsend(h, s, dev)
-    for h in range(2):
-        for r in range(2):
-            got(h, far[h] * 2 + r)
-            for dev in ways[1 - h]:
-                wsend(h, far[h] * 2 + r, dev)
-
-    def a_wait(d, carry):
-        frm = lax.rem(f + d, NF)
-        arrived(fet.at[ds(frm, CAP)], a_r.at[frm])
-        return carry
-
-    lax.fori_loop(1, NF, a_wait, 0)
+    second_near(0)
+    third(0, 0)
+
+    arrived(fet.at[pl.ds(0, PEERS * CAP)], a_r)
     share[...] = lax.dot_general(
         tt[...], fet[...], (((0,), (0,)), ((), ())), preferred_element_type=F32
     ).astype(BF16)
@@ -254,24 +283,10 @@
     keep_x = pltpu.make_async_copy(share, xwhole(c, x), loc.at[3])
     keep_x.start()
     for h in range(2):
-        half = share.at[pl.ds(h * (ROWS // 2), ROWS // 2)]
-        sends.append(rcopy(half, xpart(x, h), x_s.at[h], x_r.at[2 * x + h], tensor=x1))
-        sends.append(rcopy(half, xpart(x, h), x_s.at[2 + h], x_r.at[2 * x + h], tensor=x3))
+        rows = share.at[pl.ds(h * (ROWS // 2), ROWS // 2)]
+        sends.append(rcopy(rows, xpart(x, h), x_s.at[h], x_r.at[2 * x + h], tensor=x1))
+        sends.append(rcopy(rows, xpart(x, h), x_s.at[2 + h], x_r.at[2 * x + h], tensor=x3))
     sends.append(rcopy(share, xwhole(c, x), p_s.at[0], p_r.at[x], fsdp=mate))
-
-    def third(n):
-        yy, zz = ((y, z), (y3, z3), (y1, z1), (y2, z2))[n]
-        from_low = (at_chip(yy, z3), at_chip(y3, zz))
-        from_high = (at_chip(yy, z1), at_chip(y1, zz))
-        for h in range(2):
-            up, dn = ways[1 - h]
-            got(h, from_low[h] * 2)
-            wsend(h, from_low[h] * 2, up)
-            got(h, from_high[h] * 2 + 1)
-            wsend(h, from_high[h] * 2 + 1, dn)
-        for h in range(2):
-            got(h, from_low[h] * 2 + 1)
-            got(h, from_high[h] * 2)
 
     def x_forward():
         for h, (frm, to) in enumerate(((x3, x1), (x1, x3))):
@@ -295,17 +310,6 @@
         inv_h[ds(k, 32), :] = jnp.broadcast_to(inv, (32, 128))
         return carry
 
-    third(0)
-    x_forward()
-    third(1)
-    third(2)
-    x_finish()
-    lax.fori_loop(c * 8, c * 8 + 8, norm, 0)
-    third(3)
-    for j in (x, x3, x1, x2):
-        arrived(xwhole(1 - c, j), p_r.at[j])
-    lax.fori_loop((1 - c) * 8, (1 - c) * 8 + 8, norm, 0)
-
     def project(h, k, depth):
         acc[h] += jnp.dot(
             nrm[:, ds(k, depth)],
@@ -313,31 +317,47 @@
             preferred_element_type=F32,
         )
 
-    def near_h1(t, carry):
-        project(1, lax.rem(y + 3 + t, 4), 1024)
-        return carry
-
-    def near_h0(t, carry):
-        project(0, at_chip(lax.rem(t, 4), lax.rem(z + 3 + t // 4, 4)), 256)
-        return carry
-
-    def far_h0(t, carry):
-        project(0, at_chip(t, z2), 256)
-        return carry
+    def project_near(h):
+        def block(t, carry):
+            yy, zz = lax.rem(y + 3 + t // 3, 4), lax.rem(z + 3 + lax.rem(t, 3), 4)
+            project(h, at_chip(yy, zz), 256)
+            return carry
+
+        lax.fori_loop(0, 9, block, 0)
+
+    def project_far(h):
+        def block(t, carry):
+            yy, zz = lax.rem(y + 3 + t, 4), lax.rem(z + 3 + t, 4)
+            project(h, at_chip(yy, z2), 256)
+            project(h, at_chip(y2, zz), 256)
+            return carry
+
+        lax.fori_loop(0, 3, block, 0)
+
+    def project_last(h):
+        project(h, at_chip(y2, z2), 256)
+        qkv[:, h * TRIO : (h + 1) * TRIO] = acc[h].astype(BF16)
 
     acc[...] = jnp.zeros_like(acc)
-    lax.fori_loop(0, 3, near_h1, 0)
-    lax.fori_loop(0, 12, near_h0, 0)
-    for yy in (y, y3, y1, y2):
-        for r in range(2):
-            got(0, at_chip(yy, z2) * 2 + r)
-    lax.fori_loop(0, 4, far_h0, 0)
-    qkv[:, 0:TRIO] = acc[0].astype(BF16)
-    for zz in (z, z3, z1, z2):
-        for r in range(2):
-            got(1, at_chip(y2, zz) * 2 + r)
-    project(1, y2, 1024)
-    qkv[:, TRIO:ALL3] = acc[1].astype(BF16)
+    second_far(0)
+    third(0, 1)
+    third(0, 2)
+    x_forward()
+    third(0, 3)
+    second_near(1)
+    third(1, 0)
+    x_finish()
+    lax.fori_loop(c * 8, c * 8 + 8, norm, 0)
+    second_far(1)
+    for j in (x, x3, x1, x2):
+        arrived(xwhole(1 - c, j), p_r.at[j])
+    lax.fori_loop((1 - c) * 8, (1 - c) * 8 + 8, norm, 0)
+    project_near(0)
+    third(1, 1)
+    last(0, (0, 1, 2, 3))
+    project_far(0)
+    project_last(0)
+    third(1, 2)
 
     factor = 1.0 / math.sqrt(HEAD_DIM)
     t_row = lax.broadcasted_iota(jnp.int32, (ROWS, HEAD_DIM), 0)
@@ -347,7 +367,7 @@
     arrived(gv.at[1 - c], g_r)
 
     def attend(k, carry):
-        h, n = k // 4, lax.rem(k, 4)
+        h, n = lax.rem(k, 2), k // 2
         rows = ds(h, ROWS)
         cols = ds(n, HEAD_DIM)
         base = (n // 2) * TRIO + lax.rem(n, 2) * HEAD_DIM
@@ -366,7 +386,17 @@
         probs = raised * (1.0 / jnp.sum(raised, axis=1, keepdims=True))
         pb = probs.astype(BF16)
         out = jnp.dot(pb, vv, preferred_element_type=F32)
-        attn[rows, cols] = jnp.where(live, out, 0.0).astype(BF16)
+        out = jnp.where(live, out, 0.0).astype(BF16)
+        cols_o = pl.ds(pl.multiple_of(c * HALF + n * HEAD_DIM, HEAD_DIM), HEAD_DIM)
+
+        @pl.when(h == c)
+        def _():
+            attn_o[:, cols_o] = out
+
+        @pl.when(h != c)
+        def _():
+            attn[:, cols] = out
+
         dv = lax.dot_general(pb, gg, tn, preferred_element_type=F32).astype(BF16)
         dp = lax.dot_general(gg, vv, nt, preferred_element_type=F32)
         mid = jnp.sum(probs * dp, axis=1, keepdims=True)
@@ -385,15 +415,22 @@
         return carry
 
     stat[...] = jnp.zeros_like(stat)
-    lax.fori_loop(0, 8, attend, 0)
+    lax.fori_loop(0, 4, attend, 0)
+    third(1, 3)
+    project_near(1)
+    last(1, (0, 1, 2))
+    project_far(1)
+    last(1, (3,))
+    project_last(1)
+    lax.fori_loop(4, 8, attend, 0)
 
     rows_own, rows_mate = ds(c, ROWS), ds(1 - c, ROWS)
     low, high = pl.ds(0, ROWS // 2), pl.ds(ROWS // 2, ROWS // 2)
-    sends.append(rcopy(stat.at[rows_mate], sbuf.at[4], st_s.at[3], st_r.at[4], fsdp=mate))
+    sends.append(rcopy(stat.at[rows_mate], sbuf, st_s.at[3], st_r.at[4], fsdp=mate))
     order = (x2, x1, x3, x)
 
-    def back(u):
-        q, n = u // 4, u % 4
+    def back(q, n):
+        u = q * 4 + n
         at = pl.ds(pl.multiple_of(order[n] * WIDTH + q * UNIT, UNIT), UNIT)
         dxs[u] = lax.dot_general(grads[...], wv[at, :], nt, preferred_element_type=F32).astype(BF16)
         sends.append(rcopy(dxs.at[u, rows_mate], cbuf.at[u], c_s.at[u], c_r.at[u], fsdp=mate))
@@ -417,23 +454,17 @@
         ring(q, 3, pbuf.at[q * 4 + 2, low], rdir.at[q, 1, low], x3)
 
     def add_out(q):
-        arrived(rfwd.at[q, 0], r_r.at[q * 6])
-        u = q * 4 + 1
-        pbuf[u, low, :] = (pbuf[u, low, :].astype(F32) + rfwd[q, 0].astype(F32)).astype(BF16)
-        ring(q, 4, pbuf.at[u, low], rdir.at[q, 0, low], x1)
-        arrived(rfwd.at[q, 1], r_r.at[q * 6 + 1])
-        u = q * 4 + 2
-        pbuf[u, high, :] = (pbuf[u, high, :].astype(F32) + rfwd[q, 1].astype(F32)).astype(BF16)
-        ring(q, 5, pbuf.at[u, high], rdir.at[q, 1, high], x3)
+        for k, rows, to in ((0, low, x1), (1, high, x3)):
+            u = q * 4 + 1 + k
+            arrived(rfwd.at[q, k], r_r.at[q * 6 + k])
+            pbuf[u, rows, :] = (pbuf[u, rows, :].astype(F32) + rfwd[q, k].astype(F32)).astype(BF16)
+            ring(q, 4 + k, pbuf.at[u, rows], rdir.at[q, k, rows], to)
 
     def a_out(q):
-        arrived(rdir.at[q, 0, high], r_r.at[q * 6 + 2])
-        arrived(rdir.at[q, 1, low], r_r.at[q * 6 + 3])
-        arrived(rdir.at[q, 0, low], r_r.at[q * 6 + 4])
-        arrived(rdir.at[q, 1, high], r_r.at[q * 6 + 5])
-        iv = inv_h[rows_own, 0:1]
-        total = (sbuf[0] + sbuf[1] + sbuf[2] + sbuf[3])[:, 0:1]
-        coef = iv * iv * total / D
+        for k, rows in ((0, high), (1, low)):
+            arrived(rdir.at[q, k, rows], r_r.at[q * 6 + 2 + k])
+        for k, rows in ((0, low), (1, high)):
+            arrived(rdir.at[q, k, rows], r_r.at[q * 6 + 4 + k])
         at = pl.ds(pl.multiple_of(x * WIDTH + q * UNIT, UNIT), UNIT)
         parts = pbuf[q * 4 + 3].astype(F32) + rdir[q, 0].astype(F32) + rdir[q, 1].astype(F32)
         grad = iv * (parts * ugain[:, at]) - xh[c, :, at].astype(F32) * coef
@@ -442,7 +473,7 @@
         def send(d, carry):
             to = lax.rem(f + d, NF)
             here, there = og.at[q, ds(to, CAP)], inc.at[ds(f, CAP), pl.ds(q * UNIT, UNIT)]
-            rcopy(here, there, b_s.at[q * NF + to], b_r.at[q * NF + f], fsdp=to)
+            rcopy(here, there, b_s.at[q], b_r.at[q], fsdp=to)
             return carry
 
         lax.fori_loop(1, NF, send, 0)
@@ -452,49 +483,68 @@
         keep.start()
         return keep
 
-    back(0)
-    back(1)
+    def stat_out():
+        arrived(sbuf, st_r.at[4])
+        both = stat[rows_own, :] + sbuf[...]
+        srow[x] = jnp.transpose(both)[0:8, :]
+        for n, to in enumerate((x1, x3, x2)):
+            sends.append(rcopy(srow.at[x], srow.at[x], st_s.at[n], st_r.at[x], tensor=to))
+
+    def stat_in():
+        for frm in (x1, x3, x2):
+            arrived(srow.at[frm], st_r.at[frm])
+        total = (srow[0] + srow[1] + srow[2] + srow[3])[0:1, :]
+        full_rows = jnp.transpose(jnp.broadcast_to(total, (128, ROWS)))
+        iv = inv_h[rows_own, 0:1]
+        coef = iv * iv * full_rows[:, 0:1] / D
+        return iv, coef
+
+    for q, n in ((0, 0), (0, 1), (0, 2), (1, 0)):
+        back(q, n)
     far_out(0)
-    back(2)
-    arrived(sbuf.at[4], st_r.at[4])
-    sbuf[x] = stat[rows_own, :] + sbuf[4]
-    for n, to in enumerate((x1, x3, x2)):
-        sends.append(rcopy(sbuf.at[x], sbuf.at[x], st_s.at[n], st_r.at[x], tensor=to))
+    back(1, 1)
     near_out(0)
-    keep_a = pltpu.make_async_copy(attn.at[rows_own], attn_o.at[:, ds(c, HALF)], loc.at[12])
-    keep_a.start()
-    sends.append(rcopy(attn.at[rows_mate], attn_o.at[:, ds(c, HALF)], at_s, at_r, fsdp=mate))
-    back(3)
-    back(4)
-    back(5)
-    back(6)
+    back(1, 2)
+    far_out(1)
+    stat_out()
+    back(2, 0)
+    back(2, 1)
     add_out(0)
-    far_out(1)
     near_out(1)
-    back(7)
+    back(2, 2)
+    back(0, 3)
+    far_out(2)
+    back(3, 0)
+    back(1, 3)
+    add_out(1)
+    near_out(2)
+    back(3, 1)
+    back(3, 2)
+    far_out(3)
     summed(3)
+    iv, coef = stat_in()
+    keeps = [a_out(0)]
+    back(2, 3)
+    back(3, 3)
+    add_out(2)
+    near_out(3)
+    sends.append(rcopy(attn, attn_o.at[:, ds(c, HALF)], at_s, at_r, fsdp=mate))
     summed(7)
-    for frm in (x1, x3, x2):
-        arrived(sbuf.at[frm], st_r.at[frm])
-    add_out(1)
-    keeps = [a_out(0)]
     keeps.append(a_out(1))
-
-    def finish(d, carry):
-        frm = lax.rem(f + d, NF)
-        for q in range(2):
-            block = inc.at[ds(frm, CAP), pl.ds(q * UNIT, UNIT)]
-            arrived(block, b_r.at[q * NF + frm])
-            arrived(og.at[q, ds(frm, CAP)], b_s.at[q * NF + frm])
-        arrived(ids, id_s.at[frm])
-        arrived(fnd.at[ds(frm, CAP)], a_s.at[frm])
-        return carry
-
-    lax.fori_loop(1, NF, finish, 0)
+    add_out(3)
+    summed(11)
+    keeps.append(a_out(2))
+    summed(15)
+    keeps.append(a_out(3))
+
+    for q in range(PIECES):
+        arrived(inc.at[pl.ds(0, PEERS * CAP), pl.ds(q * UNIT, UNIT)], b_r.at[q])
+        arrived(og.at[q, pl.ds(0, PEERS * CAP)], b_s.at[q])
+    arrived(idb.at[pl.ds(0, PEERS)], id_s)
+    arrived(fnd.at[pl.ds(0, PEERS * CAP)], a_s)
     arrived(attn_o.at[:, ds(1 - c, HALF)], at_r)
     for copy in keeps:
         copy.wait()
-    keep_a.wait()
     for copy in sends:
         copy.wait_send()
 
@@ -515,7 +565,7 @@
             jax.ShapeDtypeStruct((SLOTS, WIDTH), BF16),
         ),
         in_specs=[ANY, VMEM, ANY, ANY, ANY, VMEM],
-        out_specs=(VMEM, VMEM, ANY, ANY),
+        out_specs=(VMEM, VMEM, VMEM, ANY),
         scratch_shapes=[
             vm((ROWS * ITEM_LEN, WIDTH), BF16),
             vm((NF, 8, ROWS), jnp.int32),
@@ -532,30 +582,31 @@
             vm((BOTH, ALL3), BF16),
             vm((BOTH, ALL3), BF16),
             vm((2, ROWS, HALF), BF16),
-            vm((BOTH, HALF), BF16),
+            vm((ROWS, HALF), BF16),
             vm((BOTH, 128), F32),
             vm((BOTH, 128), F32),
-            vm((5, ROWS, 128), F32),
-            vm((8, BOTH, UNIT), BF16),
-            vm((8, ROWS, UNIT), BF16),
-            vm((8, ROWS, UNIT), BF16),
-            vm((2, 2, ROWS, UNIT), BF16),
-            vm((2, 2, ROWS // 2, UNIT), BF16),
-            vm((2, SLOTS, UNIT), BF16),
-            DMA((13,)),
-            DMA((NF,)), DMA((NF,)),
+            vm((ROWS, 128), F32),
+            vm((NX, 8, ROWS), F32),
+            vm((4 * PIECES, BOTH, UNIT), BF16),
+            vm((4 * PIECES, ROWS, UNIT), BF16),
+            vm((4 * PIECES, ROWS, UNIT), BF16),
+            vm((PIECES, 2, ROWS, UNIT), BF16),
+            vm((PIECES, 2, ROWS // 2, UNIT), BF16),
+            vm((PIECES, SLOTS, UNIT), BF16),
+            DMA((10 + PIECES,)),
+            DMA, DMA,
             DMA((3,)), DMA((NX,)),
-            DMA((NF,)), DMA((NF,)),
-            DMA((64,)), DMA((2 * NF,)),
+            DMA, DMA,
+            DMA((80,)), DMA((4 * NF,)),
             DMA((6,)), DMA((6,)),
             DMA((6,)), DMA((2 * NX,)),
             DMA((4,)), DMA((NX,)),
             DMA, DMA,
             DMA, DMA,
             DMA((4,)), DMA((5,)),
-            DMA((8,)), DMA((8,)),
-            DMA((12,)), DMA((12,)),
-            DMA((2 * NF,)), DMA((2 * NF,)),
+            DMA((4 * PIECES,)), DMA((4 * PIECES,)),
+            DMA((6 * PIECES,)), DMA((6 * PIECES,)),
+            DMA((PIECES,)), DMA((PIECES,)),
         ],
         compiler_params=pltpu.CompilerParams(
             collective_id=0, has_side_effects=True, vmem_limit_bytes=62 * MIB
@@ -563,6 +614,46 @@
         cost_estimate=pl.CostEstimate(flops=27 * 10**9, bytes_accessed=64 * MIB, transcendentals=10**6),
         name="layer",
     )(item_hidden, item_gain, wqkv, ids, grad_out, user_gain)
+
+
+def closing_kernel(emb, attn, oh, inc, emb_o, attn_o, grads_o, oh_v, inc_v, emb_v, attn_v, sem):
+    pairs = ((oh, oh_v), (inc, inc_v), (emb, emb_v), (attn, attn_v), (emb_v, emb_o), (attn_v, attn_o))
+    copies = [pltpu.make_async_copy(src, dst, sem.at[n]) for n, (src, dst) in enumerate(pairs)]
+    for copy in copies[:4]:
+        copy.start()
+    for n in (2, 3):
+        copies[n].wait()
+        copies[n + 2].start()
+    for copy in copies[:2]:
+        copy.wait()
+    grads_o[...] = lax.dot_general(
+        oh_v[...], inc_v[...], (((0,), (0,)), ((), ())), preferred_element_type=F32
+    )
+    for copy in copies[4:]:
+        copy.wait()
+
+
+def closing(item_embed, attended, wanted, incoming):
+    return pl.pallas_call(
+        closing_kernel,
+        out_shape=(
+            jax.ShapeDtypeStruct((ROWS, WIDTH), BF16),
+            jax.ShapeDtypeStruct((ROWS, WIDTH), BF16),
+            jax.ShapeDtypeStruct((ROWS, WIDTH), F32),
+        ),
+        in_specs=[ANY] * 4,
+        out_specs=(ANY, ANY, VMEM),
+        scratch_shapes=[
+            pltpu.VMEM((SLOTS, ROWS), BF16),
+            pltpu.VMEM((SLOTS, WIDTH), BF16),
+            pltpu.VMEM((ROWS, WIDTH), BF16),
+            pltpu.VMEM((ROWS, WIDTH), BF16),
+            DMA((6,)),
+        ],
+        compiler_params=pltpu.CompilerParams(vmem_limit_bytes=62 * MIB),
+        cost_estimate=pl.CostEstimate(flops=3 * 10**8, bytes_accessed=5 * MIB, transcendentals=0),
+        name="closing",
+    )(item_embed, attended, wanted, incoming)
 
 
 def on_device(item_hidden, item_gain, occ_owner, occ_item, hist_len, user_gain, wqkv, grad_out):
@@ -573,10 +664,7 @@
     item_embed, wanted, attended, incoming = layer(
         item_hidden, item_gain.reshape(1, WIDTH), wqkv, ids, grad_out, user_gain.reshape(1, D)
     )
-    item_grads = lax.dot_general(
-        wanted, incoming, (((0,), (0,)), ((), ())), preferred_element_type=F32
-    )
-    return (item_embed, attended, item_grads)
+    return closing(item_embed, attended, wanted, incoming)
 
 
 def solution(mesh):

time: 155 us -> 143 us (0.923)
  Pallas kernels: 145 us -> 140 us
  local copies, waits for them, and re-layouts: 5.05 us -> 1.32 us
  matrix products: 2.76 us -> 0 us
    pallas_call x1, Pallas kernels: 145 us -> 137 us  [layer(): pl.pallas_call(layer_kernel, out_shape=(jax.ShapeDtypeStruct((ROWS, WIDTH...]
    unnamed x2 -> x0, local copies, waits for them, and re-layouts: 3.73 us -> none
    pallas_call x0 -> x1, Pallas kernels: none -> 3.43 us  [closing(): pl.pallas_call(closing_kernel, out_shape=(jax.ShapeDtypeStruct((ROWS, WID...]
    dot_general x1 -> x0, matrix products: 2.76 us -> none  [on_device(): lax.dot_general(wanted, incoming, (((0,), (0,)), ((), ())), preferred_ele...]
where the time goes in v3:
time: 143 us
  Pallas kernels  140 us (98%)
  between operations  1.47 us (1%)
    pallas_call x1, Pallas kernels, layer(): pl.pallas_call(layer_kernel, out_shape=(jax.ShapeDtypeStruct((ROWS, WIDTH...  137 us
    pallas_call x1, Pallas kernels, closing(): pl.pallas_call(closing_kernel, out_shape=(jax.ShapeDtypeStruct((ROWS, WID...  3.43 us

profile of v3, /device:TPU:1, one launch (start us, length us, event | category | flops | bytes accessed | tf_op | source)
XLA Modules:
  0.0 142.7 jit_solution(3094736903175075868)
XLA Ops:
  1.3 1.3 stack.11.ids
  2.6 136.5 %layer.1 = (bf16[256,1024]{1,0:T(8,128)(2,1)}, bf16[512,256]{1,0:T(8,128)(2,1)}, bf16[256,1024]{1,0:T(8,128)(2,1)}, bf16[512,1024]{1,0:T(8,128)(2,1)}) custom-call(bf16[2048,1024]{1,0:T(8,128)(2,1)} %hid.1, f32[1,1024]{1,0:T(1,128)} %bitcast.9, bf16[3,128,1024]{2,1,0:T(8,128)(2,1)} %w.1, s32[8,256]{1,0:T(8,128)} %stack.11.ids, bf16[256,1024]{1,0:T(8,128)(2,1)} %g.1, ...), custom_call_target="tpu_custom_call" | custom-call | flops 27000000512 | bytes 67108864 | tf_op jit(solution)/shard_map/layer/pallas_call | solution.py:559
  139.2 3.4 %closing.1 = (bf16[256,1024]{1,0:T(8,128)(2,1)}, bf16[256,1024]{1,0:T(8,128)(2,1)}, f32[256,1024]{1,0:T(8,128)}) custom-call(bf16[256,1024]{1,0:T(8,128)(2,1)} %get-tuple-element.7.emb, bf16[256,1024]{1,0:T(8,128)(2,1)} %get-tuple-element.8.attn, bf16[512,256]{1,0:T(8,128)(2,1)} %get-tuple-element.9.oh, bf16[512,1024]{1,0:T(8,128)(2,1)} %get-tuple-element.10.inc), custom_call_target="tpu_custom_call" | custom-call | flops 300000000 | bytes 5242880 | tf_op jit(solution)/shard_map/closing/pallas_call | solution.py:637
  (3 shorter events, 0.0 us)

commit v4 on v3

--- a/solution.py
+++ b/solution.py
@@ -81,7 +81,7 @@
     emb_o, oh_o, attn_o, inc,
     hid_v, idb, sqb, inv_v, tt, fnd, fet, share,
     wv, xh, nrm, acc, qkv, grads, gv, attn, inv_h, stat, sbuf, srow,
-    dxs, cbuf, pbuf, rdir, rfwd, og,
+    dx0, dxs, cbuf, pbuf, rdir, rfwd, og,
     loc, id_s, id_r, sq_s, sq_r, a_s, a_r, w_s, w_r, wm_s, wm_r,
     x_s, x_r, p_s, p_r, g_s, g_r, at_s, at_r, st_s, st_r,
     c_s, c_r, r_s, r_r, b_s, b_r,
@@ -117,14 +117,12 @@
     keep_g.start()
     greet()
 
-    load_hid.wait()
     lane = lax.broadcasted_iota(jnp.int32, (128, 128), 1)
 
     def squares(k, total):
         v = hid_v[ds(k, 128), :].astype(F32)
         return jnp.where(lane == k, jnp.sum(v * v, axis=1, keepdims=True), total)
 
-    sqb[x] = lax.fori_loop(0, 16, squares, jnp.zeros((128, 128), F32))
     greeted()
 
     def piece(h, s):
@@ -172,6 +170,8 @@
             copy.wait()
         full(h, f, first)
         full(h, f, second)
+    load_hid.wait()
+    sqb[x] = lax.fori_loop(0, 16, squares, jnp.zeros((128, 128), F32))
     for n, to in enumerate((x1, x3, x2)):
         sends.append(rcopy(sqb.at[x], sqb.at[x], sq_s.at[n], sq_r.at[x], tensor=to))
 
@@ -310,33 +310,31 @@
         inv_h[ds(k, 32), :] = jnp.broadcast_to(inv, (32, 128))
         return carry
 
-    def project(h, k, depth):
-        acc[h] += jnp.dot(
-            nrm[:, ds(k, depth)],
-            wv[ds(k, depth), h * TRIO : (h + 1) * TRIO],
-            preferred_element_type=F32,
-        )
-
-    def project_near(h):
+    def project(k):
+        acc[...] += jnp.dot(
+            nrm[:, ds(k, 256)], wv[ds(k, 256), TRIO:ALL3], preferred_element_type=F32
+        )
+
+    def project_near():
         def block(t, carry):
             yy, zz = lax.rem(y + 3 + t // 3, 4), lax.rem(z + 3 + lax.rem(t, 3), 4)
-            project(h, at_chip(yy, zz), 256)
+            project(at_chip(yy, zz))
             return carry
 
         lax.fori_loop(0, 9, block, 0)
 
-    def project_far(h):
+    def project_far():
         def block(t, carry):
             yy, zz = lax.rem(y + 3 + t, 4), lax.rem(z + 3 + t, 4)
-            project(h, at_chip(yy, z2), 256)
-            project(h, at_chip(y2, zz), 256)
+            project(at_chip(yy, z2))
+            project(at_chip(y2, zz))
             return carry
 
         lax.fori_loop(0, 3, block, 0)
 
-    def project_last(h):
-        project(h, at_chip(y2, z2), 256)
-        qkv[:, h * TRIO : (h + 1) * TRIO] = acc[h].astype(BF16)
+    def project_last():
+        project(at_chip(y2, z2))
+        qkv[:, TRIO:ALL3] = acc[...].astype(BF16)
 
     acc[...] = jnp.zeros_like(acc)
     second_far(0)
@@ -352,12 +350,15 @@
     for j in (x, x3, x1, x2):
         arrived(xwhole(1 - c, j), p_r.at[j])
     lax.fori_loop((1 - c) * 8, (1 - c) * 8 + 8, norm, 0)
-    project_near(0)
+    last(0, (0, 1, 2, 3))
+
+    def project_all(n, carry):
+        at = ds(n, GROUP)
+        qkv[:, at] = jnp.dot(nrm[...], wv[:, at], preferred_element_type=F32).astype(BF16)
+        return carry
+
+    lax.fori_loop(0, 3, project_all, 0)
     third(1, 1)
-    last(0, (0, 1, 2, 3))
-    project_far(0)
-    project_last(0)
-    third(1, 2)
 
     factor = 1.0 / math.sqrt(HEAD_DIM)
     t_row = lax.broadcasted_iota(jnp.int32, (ROWS, HEAD_DIM), 0)
@@ -415,24 +416,34 @@
         return carry
 
     stat[...] = jnp.zeros_like(stat)
-    lax.fori_loop(0, 4, attend, 0)
+    lax.fori_loop(0, 4, attend, 0, unroll=2)
+    third(1, 2)
+    def early(k, carry):
+        dx0[k] = lax.dot_general(
+            grads[:, 0:TRIO], wv[ds(k, UNIT), 0:TRIO], nt, preferred_element_type=F32
+        )
+        return carry
+
+    lax.fori_loop(0, D // UNIT, early, 0)
     third(1, 3)
-    project_near(1)
+    project_near()
     last(1, (0, 1, 2))
-    project_far(1)
+    project_far()
     last(1, (3,))
-    project_last(1)
-    lax.fori_loop(4, 8, attend, 0)
+    project_last()
+    lax.fori_loop(4, 8, attend, 0, unroll=4)
 
     rows_own, rows_mate = ds(c, ROWS), ds(1 - c, ROWS)
     low, high = pl.ds(0, ROWS // 2), pl.ds(ROWS // 2, ROWS // 2)
-    sends.append(rcopy(stat.at[rows_mate], sbuf, st_s.at[3], st_r.at[4], fsdp=mate))
     order = (x2, x1, x3, x)
 
     def back(q, n):
         u = q * 4 + n
         at = pl.ds(pl.multiple_of(order[n] * WIDTH + q * UNIT, UNIT), UNIT)
-        dxs[u] = lax.dot_general(grads[...], wv[at, :], nt, preferred_element_type=F32).astype(BF16)
+        late = lax.dot_general(
+            grads[:, TRIO:ALL3], wv[at, TRIO:ALL3], nt, preferred_element_type=F32
+        )
+        dxs[u] = (late + dx0[order[n] * PIECES + q]).astype(BF16)
         sends.append(rcopy(dxs.at[u, rows_mate], cbuf.at[u], c_s.at[u], c_r.at[u], fsdp=mate))
 
     def summed(u):
@@ -501,6 +512,7 @@
 
     for q, n in ((0, 0), (0, 1), (0, 2), (1, 0)):
         back(q, n)
+    sends.append(rcopy(stat.at[rows_mate], sbuf, st_s.at[3], st_r.at[4], fsdp=mate))
     far_out(0)
     back(1, 1)
     near_out(0)
@@ -578,7 +590,7 @@
             vm((D, ALL3), BF16),
             vm((2, ROWS, D), BF16),
             vm((BOTH, D), BF16),
-            vm((2, BOTH, TRIO), F32),
+            vm((BOTH, TRIO), F32),
             vm((BOTH, ALL3), BF16),
             vm((BOTH, ALL3), BF16),
             vm((2, ROWS, HALF), BF16),
@@ -587,6 +599,7 @@
             vm((BOTH, 128), F32),
             vm((ROWS, 128), F32),
             vm((NX, 8, ROWS), F32),
+            vm((4 * PIECES, BOTH, UNIT), F32),
             vm((4 * PIECES, BOTH, UNIT), BF16),
             vm((4 * PIECES, ROWS, UNIT), BF16),
             vm((4 * PIECES, ROWS, UNIT), BF16),

time: 143 us -> 139 us (0.972)
  Pallas kernels: 140 us -> 136 us
    pallas_call x1, Pallas kernels: 137 us -> 133 us  [layer(): pl.pallas_call(layer_kernel, out_shape=(jax.ShapeDtypeStruct((ROWS, WIDTH...]
where the time goes in v4:
time: 139 us
  Pallas kernels  136 us (98%)
  between operations  1.47 us (1%)
    pallas_call x1, Pallas kernels, layer(): pl.pallas_call(layer_kernel, out_shape=(jax.ShapeDtypeStruct((ROWS, WIDTH...  133 us
    pallas_call x1, Pallas kernels, closing(): pl.pallas_call(closing_kernel, out_shape=(jax.ShapeDtypeStruct((ROWS, WID...  3.43 us

profile of v4, /device:TPU:1, one launch (start us, length us, event | category | flops | bytes accessed | tf_op | source)
XLA Modules:
  0.0 138.8 jit_solution(15526417432689174274)
XLA Ops:
  1.3 1.3 stack.11.ids
  2.6 132.6 %layer.1 = (bf16[256,1024]{1,0:T(8,128)(2,1)}, bf16[512,256]{1,0:T(8,128)(2,1)}, bf16[256,1024]{1,0:T(8,128)(2,1)}, bf16[512,1024]{1,0:T(8,128)(2,1)}) custom-call(bf16[2048,1024]{1,0:T(8,128)(2,1)} %hid.1, f32[1,1024]{1,0:T(1,128)} %bitcast.9, bf16[3,128,1024]{2,1,0:T(8,128)(2,1)} %w.1, s32[8,256]{1,0:T(8,128)} %stack.11.ids, bf16[256,1024]{1,0:T(8,128)(2,1)} %g.1, ...), custom_call_target="tpu_custom_call" | custom-call | flops 27000000512 | bytes 67108864 | tf_op jit(solution)/shard_map/layer/pallas_call | solution.py:571
  135.2 3.4 %closing.1 = (bf16[256,1024]{1,0:T(8,128)(2,1)}, bf16[256,1024]{1,0:T(8,128)(2,1)}, f32[256,1024]{1,0:T(8,128)}) custom-call(bf16[256,1024]{1,0:T(8,128)(2,1)} %get-tuple-element.7.emb, bf16[256,1024]{1,0:T(8,128)(2,1)} %get-tuple-element.8.attn, bf16[512,256]{1,0:T(8,128)(2,1)} %get-tuple-element.9.oh, bf16[512,1024]{1,0:T(8,128)(2,1)} %get-tuple-element.10.inc), custom_call_target="tpu_custom_call" | custom-call | flops 300000000 | bytes 5242880 | tf_op jit(solution)/shard_map/closing/pallas_call | solution.py:650
  (3 shorter events, 0.0 us)

commit v5 on v4

--- a/solution.py
+++ b/solution.py
@@ -321,7 +321,7 @@
             project(at_chip(yy, zz))
             return carry
 
-        lax.fori_loop(0, 9, block, 0)
+        lax.fori_loop(0, 9, block, 0, unroll=3)
 
     def project_far():
         def block(t, carry):
@@ -424,7 +424,7 @@
         )
         return carry
 
-    lax.fori_loop(0, D // UNIT, early, 0)
+    lax.fori_loop(0, D // UNIT, early, 0, unroll=4)
     third(1, 3)
     project_near()
     last(1, (0, 1, 2))
@@ -510,9 +510,11 @@
         coef = iv * iv * full_rows[:, 0:1] / D
         return iv, coef
 
-    for q, n in ((0, 0), (0, 1), (0, 2), (1, 0)):
-        back(q, n)
+    back(0, 0)
+    back(0, 1)
+    back(0, 2)
     sends.append(rcopy(stat.at[rows_mate], sbuf, st_s.at[3], st_r.at[4], fsdp=mate))
+    back(1, 0)
     far_out(0)
     back(1, 1)
     near_out(0)
@@ -521,33 +523,34 @@
     stat_out()
     back(2, 0)
     back(2, 1)
+    back(2, 2)
     add_out(0)
     near_out(1)
-    back(2, 2)
+    far_out(2)
     back(0, 3)
-    far_out(2)
     back(3, 0)
-    back(1, 3)
+    summed(3)
+    back(3, 1)
+    back(3, 2)
     add_out(1)
     near_out(2)
-    back(3, 1)
-    back(3, 2)
+    iv, coef = stat_in()
+    keeps = []
     far_out(3)
-    summed(3)
-    iv, coef = stat_in()
-    keeps = [a_out(0)]
+    keeps.append(a_out(0))
+    back(1, 3)
     back(2, 3)
-    back(3, 3)
+    summed(7)
     add_out(2)
     near_out(3)
-    sends.append(rcopy(attn, attn_o.at[:, ds(c, HALF)], at_s, at_r, fsdp=mate))
-    summed(7)
     keeps.append(a_out(1))
+    back(3, 3)
+    summed(11)
     add_out(3)
-    summed(11)
     keeps.append(a_out(2))
     summed(15)
     keeps.append(a_out(3))
+    sends.append(rcopy(attn, attn_o.at[:, ds(c, HALF)], at_s, at_r, fsdp=mate))
 
     for q in range(PIECES):
         arrived(inc.at[pl.ds(0, PEERS * CAP), pl.ds(q * UNIT, UNIT)], b_r.at[q])

time: 139 us -> 138 us (level)
  no operation moved by 1% of the time
where the time goes in v5:
time: 138 us
  Pallas kernels  135 us (98%)
  between operations  1.47 us (1%)
    pallas_call x1, Pallas kernels, layer(): pl.pallas_call(layer_kernel, out_shape=(jax.ShapeDtypeStruct((ROWS, WIDTH...  132 us
    pallas_call x1, Pallas kernels, closing(): pl.pallas_call(closing_kernel, out_shape=(jax.ShapeDtypeStruct((ROWS, WID...  3.43 us

profile of v5, /device:TPU:1, one launch (start us, length us, event | category | flops | bytes accessed | tf_op | source)
XLA Modules:
  0.0 138.1 jit_solution(8888538528143277301)
XLA Ops:
  1.3 1.3 stack.11.ids
  2.6 131.9 %layer.1 = (bf16[256,1024]{1,0:T(8,128)(2,1)}, bf16[512,256]{1,0:T(8,128)(2,1)}, bf16[256,1024]{1,0:T(8,128)(2,1)}, bf16[512,1024]{1,0:T(8,128)(2,1)}) custom-call(bf16[2048,1024]{1,0:T(8,128)(2,1)} %hid.1, f32[1,1024]{1,0:T(1,128)} %bitcast.9, bf16[3,128,1024]{2,1,0:T(8,128)(2,1)} %w.1, s32[8,256]{1,0:T(8,128)} %stack.11.ids, bf16[256,1024]{1,0:T(8,128)(2,1)} %g.1, ...), custom_call_target="tpu_custom_call" | custom-call | flops 27000000512 | bytes 67108864 | tf_op jit(solution)/shard_map/layer/pallas_call | solution.py:574
  134.5 3.4 %closing.1 = (bf16[256,1024]{1,0:T(8,128)(2,1)}, bf16[256,1024]{1,0:T(8,128)(2,1)}, f32[256,1024]{1,0:T(8,128)}) custom-call(bf16[256,1024]{1,0:T(8,128)(2,1)} %get-tuple-element.7.emb, bf16[256,1024]{1,0:T(8,128)(2,1)} %get-tuple-element.8.attn, bf16[512,256]{1,0:T(8,128)(2,1)} %get-tuple-element.9.oh, bf16[512,1024]{1,0:T(8,128)(2,1)} %get-tuple-element.10.inc), custom_call_target="tpu_custom_call" | custom-call | flops 300000000 | bytes 5242880 | tf_op jit(solution)/shard_map/closing/pallas_call | solution.py:653
  (3 shorter events, 0.0 us)
